TPU v7x, 512 devices: a whole 4x4x16 slice. The times are simulated.
512 devices in a mesh: gx: 16 (over x, z_lo), gy: 8 (over z_hi, core), gz: 4 (over y).
Axes of the slice: x: 4, y: 4, z: 16 (z_hi: 4, z_lo: 4; z = z_hi * 4 + z_lo), core: 2. Of those that a mesh axis runs over, the one named last changes fastest.
Arguments:
- offsets: float32 [3, 32, 16, 8, 128], P(None, 'gx', 'gy', 'gz'), may hold values from 0 to 1
- velocities: float32 [3, 32, 16, 8, 128], P(None, 'gx', 'gy', 'gz'), may hold values from -3 to 3
- smoothing: float32 [32, 16, 8, 128], P('gx', 'gy', 'gz'), may hold values from 0.6 to 1
- mass: float32 [32, 16, 8, 128], P('gx', 'gy', 'gz'), may hold values from 0.004 to 0.016
- entropy: float32 [32, 16, 8, 128], P('gx', 'gy', 'gz'), may hold values from 0.5 to 2
- prior_density: float32 [32, 16, 8, 128], P('gx', 'gy', 'gz'), may hold values from 0.5 to 2
- active: int32 [32, 16, 8, 128], P('gx', 'gy', 'gz'), may hold values from 0 to 1, as said below
Outputs:
- density: float32 [32, 16, 8, 128], P('gx', 'gy', 'gz')
- acceleration: float32 [3, 32, 16, 8, 128], P(None, 'gx', 'gy', 'gz')
Inputs may be any that keep to these rules, and one draw needn't show every extreme that they name: 1 marks an active particle; activity is set in aligned blocks of 2 x 2 x 2 cells, and some blocks hold no active particle.
All inputs are finite; a program needn't handle non-finite values.
Results may differ from a plain program's by a relative error of at most 0.0001.
Values sent between devices are 32-bit elements; how exact they have to be, the bound alone decides.
A program may use at most 64 MiB of HBM per device.

v0:
```python
import math

import jax
import jax.numpy as jnp
from jax import lax
from jax.sharding import PartitionSpec as P

kernel_norm = 21.0 / (2.0 * math.pi)
visc_alpha = 1.0
visc_beta = 2.0


def extended(cells, sides, width):
    for axis, dim in sides:
        count = lax.axis_size(axis)
        head = lax.slice_in_dim(cells, 0, width, axis=dim)
        tail = lax.slice_in_dim(cells, cells.shape[dim] - width, cells.shape[dim], axis=dim)
        cells = jnp.concatenate(
            [
                lax.ppermute(tail, axis, [(i, (i + 1) % count) for i in range(count)]),
                cells,
                lax.ppermute(head, axis, [((i + 1) % count, i) for i in range(count)]),
            ],
            axis=dim,
        )
    return cells


def neighbour_shifts():
    return [
        (step_x, step_y, step_z)
        for step_x in (-1, 0, 1)
        for step_y in (-1, 0, 1)
        for step_z in (-1, 0, 1)
    ]


def kernel_terms(radius_sq, smooth):
    ratio = jnp.sqrt(radius_sq) / smooth
    inside = jnp.maximum(1.0 - ratio, 0.0)
    value = kernel_norm / smooth**3 * inside**4 * (1.0 + 4.0 * ratio)
    slope = -20.0 * kernel_norm / smooth**5 * inside**3
    return (value, slope)


def neighbour_cells(beside_all, shift, center):
    size_x, size_y, size_z = (center.shape[1], center.shape[2], center.shape[3])
    return beside_all[
        :,
        1 + shift[0] : 1 + shift[0] + size_x,
        1 + shift[1] : 1 + shift[1] + size_y,
        1 + shift[2] : 1 + shift[2] + size_z,
    ]


def separation(center, neighbour, shift):
    return [
        center[axis_id][..., :, None] - neighbour[axis_id][..., None, :] - float(shift[axis_id])
        for axis_id in range(3)
    ]


def density_block(beside_all):
    center = beside_all[:, 1:-1, 1:-1, 1:-1]
    smooth = center[6][..., :, None]
    total = jnp.zeros(center.shape[1:], jnp.float32)
    for shift in neighbour_shifts():
        neighbour = neighbour_cells(beside_all, shift, center)
        parts = separation(center, neighbour, shift)
        radius_sq = parts[0] ** 2 + parts[1] ** 2 + parts[2] ** 2
        value, slope = kernel_terms(radius_sq, smooth)
        total = total + jnp.sum(neighbour[7][..., None, :] * value, axis=-1)
    return total


def force_block(beside_all):
    center = beside_all[:, 1:-1, 1:-1, 1:-1]
    smooth_own = center[6][..., :, None]
    dens_own = center[8][..., :, None]
    factor_own = center[9][..., :, None]
    sound_own = center[10][..., :, None]
    totals = [jnp.zeros(center.shape[1:], jnp.float32) for axis_id in range(3)]
    for shift in neighbour_shifts():
        neighbour = neighbour_cells(beside_all, shift, center)
        parts = separation(center, neighbour, shift)
        radius_sq = parts[0] ** 2 + parts[1] ** 2 + parts[2] ** 2
        approach = parts[0] * (center[3][..., :, None] - neighbour[3][..., None, :])
        approach = approach + parts[1] * (center[4][..., :, None] - neighbour[4][..., None, :])
        approach = approach + parts[2] * (center[5][..., :, None] - neighbour[5][..., None, :])
        smooth_far = neighbour[6][..., None, :]
        value_own, slope_own = kernel_terms(radius_sq, smooth_own)
        value_far, slope_far = kernel_terms(radius_sq, smooth_far)
        mean_smooth = 0.5 * (smooth_own + smooth_far)
        closing = mean_smooth * jnp.minimum(approach, 0.0) / (radius_sq + 0.01 * mean_smooth**2)
        viscous = (
            -visc_alpha * 0.5 * (sound_own + neighbour[10][..., None, :]) * closing
            + visc_beta * closing**2
        ) / (0.5 * (dens_own + neighbour[8][..., None, :]))
        weight = neighbour[7][..., None, :] * (
            factor_own * slope_own
            + neighbour[9][..., None, :] * slope_far
            + viscous * 0.5 * (slope_own + slope_far)
        )
        for axis_id in range(3):
            totals[axis_id] = totals[axis_id] - jnp.sum(weight * parts[axis_id], axis=-1)
    return jnp.stack(totals)


def ghost_cells(payload, width):
    return extended(payload, (("gx", 1), ("gy", 2), ("gz", 3)), width)


def pressure_terms(entropy, density):
    factor = entropy * density ** (-1.0 / 3.0)
    sound = jnp.sqrt(5.0 / 3.0 * entropy * density ** (2.0 / 3.0))
    return (factor, sound)


def body(offsets, velocities, smoothing, mass, entropy, prior_density, active):
    fields = jnp.concatenate(
        [offsets, velocities, smoothing[None], mass[None], entropy[None]], axis=0
    )
    beside_all = ghost_cells(fields, 1)
    computed = density_block(beside_all)
    density = jnp.where(active == 1, computed, prior_density)
    cycle_density = ghost_cells(density[None], 1)[0]
    factor, sound = pressure_terms(beside_all[8], cycle_density)
    force_around = jnp.concatenate(
        [beside_all[:8], cycle_density[None], factor[None], sound[None]], axis=0
    )
    accel = force_block(force_around)
    accel = jnp.where(active[None] == 1, accel, 0.0)
    return (density, accel)


def solution(mesh):
    in_specs = (
        P(None, "gx", "gy", "gz", None),
        P(None, "gx", "gy", "gz", None),
        P("gx", "gy", "gz", None),
        P("gx", "gy", "gz", None),
        P("gx", "gy", "gz", None),
        P("gx", "gy", "gz", None),
        P("gx", "gy", "gz", None),
    )
    out_specs = (P("gx", "gy", "gz", None), P(None, "gx", "gy", "gz", None))
    return jax.shard_map(body, mesh=mesh, in_specs=in_specs, out_specs=out_specs, check_vma=False)
```

profile of v0, /device:TPU:1, one launch (start us, length us, event | category | flops | bytes accessed | tf_op | source)
XLA Modules:
  0.0 139.6 jit_solution(2416096636374588367)
XLA Ops:
  0.6 0.7 constant_dynamic-update-slice_fusion.4
  1.4 0.7 copy-done.3
  2.1 0.7 copy-done.7
  2.7 0.7 copy-done.6
  3.4 4.4 %collective-permute-start = (f32[9,1,2,2,128]{4,3,2,1,0:T(2,128)S(1)}, f32[9,1,2,2,128]{4,3,2,1,0:T(2,128)S(1)}, u32[]{:S(2)}, u32[]{:S(2)}) collective-permute-start(f32[9,1,2,2,128]{4,3,2,1,0:T(2,128)S(1)} %get-tuple-element.423), channel_id=1, source_target_pairs={{0,32},{32,64},{64,96},{96,128},{128,160},{160,192},{192,224},{224... | collective-permute-start | bytes 55304 | tf_op jit(solution)/shard_map/ppermute | solution.py:20
  7.8 6.8 %collective-permute-start.1 = (f32[9,1,2,2,128]{4,3,2,1,0:T(2,128)S(1)}, f32[9,1,2,2,128]{4,3,2,1,0:T(2,128)S(1)}, u32[]{:S(2)}, u32[]{:S(2)}) collective-permute-start(f32[9,1,2,2,128]{4,3,2,1,0:T(2,128)S(1)} %get-tuple-element.424), channel_id=1, source_target_pairs={{32,0},{64,32},{96,64},{128,96},{160,128},{192,160},{224,192},{256... | collective-permute-start | bytes 55304 | tf_op jit(solution)/shard_map/ppermute | solution.py:22
  14.7 0.8 collective-permute-done.1
  15.6 10.2 %collective-permute-start.2 = (f32[9,4,1,2,128]{4,3,2,1,0:T(2,128)S(1)}, f32[9,4,1,2,128]{4,3,2,1,0:T(2,128)S(1)}, u32[]{:S(2)}, u32[]{:S(2)}) collective-permute-start(f32[9,4,1,2,128]{4,3,2,1,0:T(2,128)S(1)} %get-tuple-element.403), channel_id=1, source_target_pairs={{0,4},{4,8},{8,12},{12,16},{16,20},{20,24},{24,28},{28,0},{1,5},{5... | collective-permute-start | bytes 110600 | tf_op jit(solution)/shard_map/ppermute | solution.py:20
  25.8 1.9 %collective-permute-start.3 = (f32[9,4,1,2,128]{4,3,2,1,0:T(2,128)S(1)}, f32[9,4,1,2,128]{4,3,2,1,0:T(2,128)S(1)}, u32[]{:S(2)}, u32[]{:S(2)}) collective-permute-start(f32[9,4,1,2,128]{4,3,2,1,0:T(2,128)S(1)} %get-tuple-element.404), channel_id=1, source_target_pairs={{4,0},{8,4},{12,8},{16,12},{20,16},{24,20},{28,24},{0,28},{5,1},{9... | collective-permute-start | bytes 110600 | tf_op jit(solution)/shard_map/ppermute | solution.py:22
  27.8 7.6 %collective-permute-done.3 = f32[9,4,1,2,128]{4,3,2,1,0:T(2,128)S(1)} collective-permute-done((f32[9,4,1,2,128]{4,3,2,1,0:T(2,128)S(1)}, f32[9,4,1,2,128]{4,3,2,1,0:T(2,128)S(1)}, u32[]{:S(2)}, u32[]{:S(2)}) %collective-permute-start.3) | collective-permute-done | bytes 36896 | tf_op jit(solution)/shard_map/ppermute | solution.py:22
  35.4 0.1 pad_maximum_fusion.1
  35.5 0.1 fusion.350
  35.6 3.2 %collective-permute-start.4 = (f32[9,4,4,1,128]{4,3,2,1,0:T(1,128)S(1)}, f32[9,4,4,1,128]{4,3,2,1,0:T(1,128)S(1)}, u32[]{:S(2)}, u32[]{:S(2)}) collective-permute-start(f32[9,4,4,1,128]{4,3,2,1,0:T(1,128)S(1)} %get-tuple-element.351), channel_id=1, source_target_pairs={{0,1},{1,2},{2,3},{3,0},{4,5},{5,6},{6,7},{7,4},{8,9},{9,10},{10,1... | collective-permute-start | bytes 221192 | tf_op jit(solution)/shard_map/ppermute | solution.py:20
  38.8 3.4 %collective-permute-start.5 = (f32[9,4,4,1,128]{4,3,2,1,0:T(1,128)S(1)}, f32[9,4,4,1,128]{4,3,2,1,0:T(1,128)S(1)}, u32[]{:S(2)}, u32[]{:S(2)}) collective-permute-start(f32[9,4,4,1,128]{4,3,2,1,0:T(1,128)S(1)} %get-tuple-element.352), channel_id=1, source_target_pairs={{1,0},{2,1},{3,2},{0,3},{5,4},{6,5},{7,6},{4,7},{9,8},{10,9},{11,1... | collective-permute-start | bytes 221192 | tf_op jit(solution)/shard_map/ppermute | solution.py:22
  42.5 1.4 %collective-permute-done.5 = f32[9,4,4,1,128]{4,3,2,1,0:T(1,128)S(1)} collective-permute-done((f32[9,4,4,1,128]{4,3,2,1,0:T(1,128)S(1)}, f32[9,4,4,1,128]{4,3,2,1,0:T(1,128)S(1)}, u32[]{:S(2)}, u32[]{:S(2)}) %collective-permute-start.5) | collective-permute-done | bytes 73760 | tf_op jit(solution)/shard_map/ppermute | solution.py:22
  43.9 0.3 maximum_maximum_fusion
  44.5 1.5 %fusion.128 = (f32[2,2,2,128]{3,2,1,0:T(2,128)S(1)}, f32[2,2,2,128]{3,2,1,0:T(2,128)S(1)}) fusion(f32[2,2,2,128]{3,2,1,0:T(2,128)S(1)} %get-tuple-element.380, f32[2,2,2,128]{3,2,1,0:T(2,128)S(1)} %get-tuple-element.382, f32[2,2,2,128]{3,2,1,0:T(2,128)S(1)} %get-tuple-element.383, f32[2,2,2,128]{3,2,1,0:T(2,128)S(1)} %get-tuple-element.384, ...), kind=kLoop, calls=%fused_computation.290 | loop fusion | flops 5634048 | bytes 61440 | tf_op jit(solution)/shard_map/reduce_sum | solution.py:72
  45.9 1.8 %fusion.48 = (f32[2,2,2,128]{3,2,1,0:T(2,128)S(1)}, f32[2,2,2,128]{3,2,1,0:T(2,128)S(1)}, f32[2,2,2,128]{3,2,1,0:T(2,128)S(1)}) fusion(f32[2,2,2,128]{3,2,1,0:T(2,128)S(1)} %get-tuple-element.335, f32[2,2,2,128]{3,2,1,0:T(2,128)S(1)} %get-tuple-element.336, f32[2,2,2,128]{3,2,1,0:T(2,128)S(1)} %get-tuple-element.337, ...), kind=kLoop, calls=%fused_computation.210 | loop fusion | flops 8123392 | bytes 81920 | tf_op jit(solution)/shard_map/reduce_sum | solution.py:72
  47.8 1.9 %fusion.33 = (f32[2,2,2,128]{3,2,1,0:T(2,128)S(1)}, f32[2,2,2,128]{3,2,1,0:T(2,128)S(1)}, f32[2,2,2,128]{3,2,1,0:T(2,128)S(1)}) fusion(f32[2,2,2,128]{3,2,1,0:T(2,128)S(1)} %get-tuple-element.342, f32[2,2,2,128]{3,2,1,0:T(2,128)S(1)} %copy-done.3, f32[2,2,2,128]{3,2,1,0:T(2,128)S(1)} %get-tuple-element.339, f32[2,2,2,128]{3,2,1,0:T(2,128)S(1)} %get-tuple-element.511, ...), kind=kLoop, calls=%fused_computation.195 | loop fusion | flops 8516608 | bytes 81920 | tf_op jit(solution)/shard_map/reduce_sum | solution.py:72
  49.7 2.4 %fusion.8 = (f32[2,2,2,128]{3,2,1,0:T(2,128)S(1)}, f32[2,2,2,128]{3,2,1,0:T(2,128)S(1)}, f32[2,2,2,128]{3,2,1,0:T(2,128)S(1)}, f32[2,2,2,128]{3,2,1,0:T(2,128)S(1)}) fusion(f32[2,2,2,128]{3,2,1,0:T(2,128)S(1)} %get-tuple-element.398, f32[2,2,2,128]{3,2,1,0:T(2,128)S(1)} %get-tuple-element.399, f32[2,2,2,128]{3,2,1,0:T(2,128)S(1)} %get-tuple-element.400, ...), kind=kLoop, calls=%fused_computation.170 | loop fusion | flops 10874880 | bytes 90112 | tf_op jit(solution)/shard_map/reduce_sum | solution.py:72
  52.1 1.9 %fusion.3 = (f32[2,2,2,128]{3,2,1,0:T(2,128)S(1)}, f32[2,2,2,128]{3,2,1,0:T(2,128)S(1)}, f32[2,2,2,128]{3,2,1,0:T(2,128)S(1)}) fusion(f32[2,2,2,128]{3,2,1,0:T(2,128)S(1)} %copy-done.3, f32[2,2,2,128]{3,2,1,0:T(2,128)S(1)} %get-tuple-element.347, f32[2,2,2,128]{3,2,1,0:T(2,128)S(1)} %get-tuple-element.511, f32[2,2,2,128]{3,2,1,0:T(2,128)S(1)} %get-tuple-element.348, ...), kind=kLoop, calls=%fused_computation.165 | loop fusion | flops 8254464 | bytes 81920 | tf_op jit(solution)/shard_map/reduce_sum | solution.py:72
  53.9 1.8 %fusion.113 = (f32[2,2,2,128]{3,2,1,0:T(2,128)S(1)}, f32[2,2,2,128]{3,2,1,0:T(2,128)S(1)}, f32[2,2,2,128]{3,2,1,0:T(2,128)S(1)}) fusion(f32[2,2,2,128]{3,2,1,0:T(2,128)S(1)} %get-tuple-element.419, f32[2,2,2,128]{3,2,1,0:T(2,128)S(1)} %copy-done.3, f32[2,2,2,128]{3,2,1,0:T(2,128)S(1)} %get-tuple-element.416, f32[2,2,2,128]{3,2,1,0:T(2,128)S(1)} %get-tuple-element.511, ...), kind=kLoop, calls=%fused_computation.275 | loop fusion | flops 8254464 | bytes 81920 | tf_op jit(solution)/shard_map/reduce_sum | solution.py:72
  55.8 1.9 %fusion.98 = (f32[2,2,2,128]{3,2,1,0:T(2,128)S(1)}, f32[2,2,2,128]{3,2,1,0:T(2,128)S(1)}, f32[2,2,2,128]{3,2,1,0:T(2,128)S(1)}) fusion(f32[2,2,2,128]{3,2,1,0:T(2,128)S(1)} %get-tuple-element.366, f32[2,2,2,128]{3,2,1,0:T(2,128)S(1)} %get-tuple-element.367, f32[2,2,2,128]{3,2,1,0:T(2,128)S(1)} %get-tuple-element.368, ...), kind=kLoop, calls=%fused_computation.260 | loop fusion | flops 8385536 | bytes 81920 | tf_op jit(solution)/shard_map/reduce_sum | solution.py:72
  57.6 1.9 %fusion.83 = (f32[2,2,2,128]{3,2,1,0:T(2,128)S(1)}, f32[2,2,2,128]{3,2,1,0:T(2,128)S(1)}, f32[2,2,2,128]{3,2,1,0:T(2,128)S(1)}) fusion(f32[2,2,2,128]{3,2,1,0:T(2,128)S(1)} %get-tuple-element.390, f32[2,2,2,128]{3,2,1,0:T(2,128)S(1)} %copy-done.3, f32[2,2,2,128]{3,2,1,0:T(2,128)S(1)} %get-tuple-element.386, f32[2,2,2,128]{3,2,1,0:T(2,128)S(1)} %get-tuple-element.511, ...), kind=kLoop, calls=%fused_computation.245 | loop fusion | flops 8254464 | bytes 81920 | tf_op jit(solution)/shard_map/reduce_sum | solution.py:72
  59.5 1.8 %fusion.63 = (f32[2,2,2,128]{3,2,1,0:T(2,128)S(1)}, f32[2,2,2,128]{3,2,1,0:T(2,128)S(1)}, f32[2,2,2,128]{3,2,1,0:T(2,128)S(1)}) fusion(f32[2,2,2,128]{3,2,1,0:T(2,128)S(1)} %get-tuple-element.333, f32[2,2,2,128]{3,2,1,0:T(2,128)S(1)} %copy-done.3, f32[2,2,2,128]{3,2,1,0:T(2,128)S(1)} %get-tuple-element.330, f32[2,2,2,128]{3,2,1,0:T(2,128)S(1)} %get-tuple-element.511, ...), kind=kLoop, calls=%fused_computation.225 | loop fusion | flops 7992320 | bytes 81920 | tf_op jit(solution)/shard_map/reduce_sum | solution.py:72
  61.3 0.7 copy-done.5
  62.0 0.0 copy-done.4
  62.1 0.0 copy-start
  62.1 1.9 %collective-permute-start.6 = (f32[1,1,2,2,128]{4,3,2,1,0:T(2,128)S(1)}, f32[1,1,2,2,128]{4,3,2,1,0:T(2,128)S(1)}, u32[]{:S(2)}, u32[]{:S(2)}) collective-permute-start(f32[1,1,2,2,128]{4,3,2,1,0:T(2,128)S(1)} %get-tuple-element.521), channel_id=1, source_target_pairs={{0,32},{32,64},{64,96},{96,128},{128,160},{160,192},{192,224},{224... | collective-permute-start | bytes 6152 | tf_op jit(solution)/shard_map/ppermute | solution.py:20
  64.0 8.6 %collective-permute-start.7 = (f32[1,1,2,2,128]{4,3,2,1,0:T(2,128)S(1)}, f32[1,1,2,2,128]{4,3,2,1,0:T(2,128)S(1)}, u32[]{:S(2)}, u32[]{:S(2)}) collective-permute-start(f32[1,1,2,2,128]{4,3,2,1,0:T(2,128)S(1)} %get-tuple-element.522), channel_id=1, source_target_pairs={{32,0},{64,32},{96,64},{128,96},{160,128},{192,160},{224,192},{256... | collective-permute-start | bytes 6152 | tf_op jit(solution)/shard_map/ppermute | solution.py:22
  72.7 0.7 collective-permute-done.7
  73.4 3.0 %collective-permute-start.8 = (f32[1,4,1,2,128]{4,3,2,1,0:T(2,128)S(1)}, f32[1,4,1,2,128]{4,3,2,1,0:T(2,128)S(1)}, u32[]{:S(2)}, u32[]{:S(2)}) collective-permute-start(f32[1,4,1,2,128]{4,3,2,1,0:T(2,128)S(1)} %get-tuple-element.515), channel_id=1, source_target_pairs={{0,4},{4,8},{8,12},{12,16},{16,20},{20,24},{24,28},{28,0},{1,5},{5... | collective-permute-start | bytes 12296 | tf_op jit(solution)/shard_map/ppermute | solution.py:20
  76.4 1.9 %collective-permute-start.9 = (f32[1,4,1,2,128]{4,3,2,1,0:T(2,128)S(1)}, f32[1,4,1,2,128]{4,3,2,1,0:T(2,128)S(1)}, u32[]{:S(2)}, u32[]{:S(2)}) collective-permute-start(f32[1,4,1,2,128]{4,3,2,1,0:T(2,128)S(1)} %get-tuple-element.516), channel_id=1, source_target_pairs={{4,0},{8,4},{12,8},{16,12},{20,16},{24,20},{28,24},{0,28},{5,1},{9... | collective-permute-start | bytes 12296 | tf_op jit(solution)/shard_map/ppermute | solution.py:22
  78.3 6.9 %collective-permute-done.9 = f32[1,4,1,2,128]{4,3,2,1,0:T(2,128)S(1)} collective-permute-done((f32[1,4,1,2,128]{4,3,2,1,0:T(2,128)S(1)}, f32[1,4,1,2,128]{4,3,2,1,0:T(2,128)S(1)}, u32[]{:S(2)}, u32[]{:S(2)}) %collective-permute-start.9) | collective-permute-done | bytes 4128 | tf_op jit(solution)/shard_map/ppermute | solution.py:22
  85.3 3.2 %collective-permute-start.10 = (f32[1,4,4,1,128]{4,3,2,1,0:T(1,128)S(1)}, f32[1,4,4,1,128]{4,3,2,1,0:T(1,128)S(1)}, u32[]{:S(2)}, u32[]{:S(2)}) collective-permute-start(f32[1,4,4,1,128]{4,3,2,1,0:T(1,128)S(1)} %get-tuple-element.499), channel_id=1, source_target_pairs={{0,1},{1,2},{2,3},{3,0},{4,5},{5,6},{6,7},{7,4},{8,9},{9,10},{10,1... | collective-permute-start | bytes 24584 | tf_op jit(solution)/shard_map/ppermute | solution.py:20
  88.5 3.3 %collective-permute-start.11 = (f32[1,4,4,1,128]{4,3,2,1,0:T(1,128)S(1)}, f32[1,4,4,1,128]{4,3,2,1,0:T(1,128)S(1)}, u32[]{:S(2)}, u32[]{:S(2)}) collective-permute-start(f32[1,4,4,1,128]{4,3,2,1,0:T(1,128)S(1)} %get-tuple-element.500), channel_id=1, source_target_pairs={{1,0},{2,1},{3,2},{0,3},{5,4},{6,5},{7,6},{4,7},{9,8},{10,9},{11,1... | collective-permute-start | bytes 24584 | tf_op jit(solution)/shard_map/ppermute | solution.py:22
  91.8 1.1 collective-permute-done.11
  92.9 0.1 power_multiply_fusion
  93.0 0.1 multiply_sqrt_fusion
  93.3 2.7 %multiply_reduce_fusion.42 = (f32[2,2,2,128]{3,2,1,0:T(2,128)S(1)}, f32[2,2,2,128]{3,2,1,0:T(2,128)S(1)}, f32[2,2,2,128]{3,2,1,0:T(2,128)S(1)}) fusion(f32[2,2,2,128]{3,2,1,0:T(2,128)S(1)} %get-tuple-element.290, f32[2,2,2,128]{3,2,1,0:T(2,128)S(1)} %get-tuple-element.510, f32[2,2,2,128]{3,2,1,0:T(2,128)S(1)} %get-tuple-element.288, ...), kind=kLoop, calls=%fused_computation.526 | loop fusion | flops 8123392 | bytes 106496 | tf_op jit(solution)/shard_map/reduce_sum | solution.py:105
  96.0 3.6 %fusion.240 = (f32[2,2,2,128]{3,2,1,0:T(2,128)S(1)}, f32[2,2,2,128]{3,2,1,0:T(2,128)S(1)}, f32[2,2,2,128]{3,2,1,0:T(2,128)S(1)}, f32[2,2,2,128]{3,2,1,0:T(2,128)...) fusion(f32[2,2,2,128]{3,2,1,0:T(2,128)S(1)} %get-tuple-element.510, ...), kind=kLoop, calls=%fused_computation.402 | loop fusion | flops 15853568 | bytes 122880 | tf_op jit(solution)/shard_map/reduce_sum | solution.py:105
  99.6 6.6 %multiply_reduce_fusion.41 = (f32[2,2,2,128]{3,2,1,0:T(2,128)S(1)}, f32[2,2,2,128]{3,2,1,0:T(2,128)S(1)}, f32[2,2,2,128]{3,2,1,0:T(2,128)S(1)}, f32[2,2,2,128]{3...) fusion(f32[2,2,2,128]{3,2,1,0:T(2,128)S(1)} %get-tuple-element., ...), kind=kLoop, calls=%fused_computation.524 | loop fusion | flops 32100352 | bytes 290816 | tf_op jit(solution)/shard_map/reduce_sum | solution.py:105
  106.2 6.5 %multiply_reduce_fusion.40 = (f32[2,2,2,128]{3,2,1,0:T(2,128)S(1)}, f32[2,2,2,128]{3,2,1,0:T(2,128)S(1)}, f32[2,2,2,128]{3,2,1,0:T(2,128)S(1)}, f32[2,2,2,128]{3...) fusion(f32[2,2,2,128]{3,2,1,0:T(2,128)S(1)} %get-tuple-element., ...), kind=kLoop, calls=%fused_computation.522 | loop fusion | flops 31576064 | bytes 290816 | tf_op jit(solution)/shard_map/reduce_sum | solution.py:105
  112.7 6.5 %multiply_reduce_fusion.39 = (f32[2,2,2,128]{3,2,1,0:T(2,128)S(1)}, f32[2,2,2,128]{3,2,1,0:T(2,128)S(1)}, f32[2,2,2,128]{3,2,1,0:T(2,128)S(1)}, f32[2,2,2,128]{3...) fusion(f32[2,2,2,128]{3,2,1,0:T(2,128)S(1)} %get-tuple-element., ...), kind=kLoop, calls=%fused_computation.520 | loop fusion | flops 31707136 | bytes 290816 | tf_op jit(solution)/shard_map/reduce_sum | solution.py:105
  119.2 6.6 %multiply_reduce_fusion.38 = (f32[2,2,2,128]{3,2,1,0:T(2,128)S(1)}, f32[2,2,2,128]{3,2,1,0:T(2,128)S(1)}, f32[2,2,2,128]{3,2,1,0:T(2,128)S(1)}, f32[2,2,2,128]{3...) fusion(f32[2,2,2,128]{3,2,1,0:T(2,128)S(1)} %get-tuple-element., ...), kind=kLoop, calls=%fused_computation.518 | loop fusion | flops 32231424 | bytes 290816 | tf_op jit(solution)/shard_map/reduce_sum | solution.py:105
  125.8 6.5 %multiply_reduce_fusion.37 = (f32[2,2,2,128]{3,2,1,0:T(2,128)S(1)}, f32[2,2,2,128]{3,2,1,0:T(2,128)S(1)}, f32[2,2,2,128]{3,2,1,0:T(2,128)S(1)}, f32[2,2,2,128]{3...) fusion(f32[2,2,2,128]{3,2,1,0:T(2,128)S(1)} %get-tuple-element., ...), kind=kLoop, calls=%fused_computation.516 | loop fusion | flops 31969280 | bytes 290816 | tf_op jit(solution)/shard_map/reduce_sum | solution.py:105
  132.3 6.6 %multiply_reduce_fusion.36 = (f32[2,2,2,128]{3,2,1,0:T(2,128)S(1)}, f32[2,2,2,128]{3,2,1,0:T(2,128)S(1)}, f32[2,2,2,128]{3,2,1,0:T(2,128)S(1)}, f32[2,2,2,128]{3...) fusion(f32[2,2,2,128]{3,2,1,0:T(2,128)S(1)} %get-tuple-element., ...), kind=kLoop, calls=%fused_computation.514 | loop fusion | flops 32231424 | bytes 290816 | tf_op jit(solution)/shard_map/reduce_sum | solution.py:105
  139.0 0.6 maximum_select_fusion
  (66 shorter events, 1.0 us)
Async XLA Ops:
  0.6 0.7 copy-start.2
  1.4 0.7 copy-start.3
  2.0 0.7 copy-start.7
  2.7 0.7 copy-start.6
  3.4 11.2 %copy-start.1 = (f32[3,2,2,2,128]{4,3,2,1,0:T(2,128)S(1)}, f32[3,2,2,2,128]{4,3,2,1,0:T(2,128)}, u32[]{:S(2)}) copy-start(f32[3,2,2,2,128]{4,3,2,1,0:T(2,128)} %param.7) | copy-start | bytes 36868
  3.4 11.3 %collective-permute-start = (f32[9,1,2,2,128]{4,3,2,1,0:T(2,128)S(1)}, f32[9,1,2,2,128]{4,3,2,1,0:T(2,128)S(1)}, u32[]{:S(2)}, u32[]{:S(2)}) collective-permute-start(f32[9,1,2,2,128]{4,3,2,1,0:T(2,128)S(1)} %get-tuple-element.423), channel_id=1, source_target_pairs={{0,32},{32,64},{64,96},{96,128},{128,160},{160,192},{192,224},{224... | collective-permute-start | bytes 55304 | tf_op jit(solution)/shard_map/ppermute | solution.py:20
  7.8 7.7 %collective-permute-start.1 = (f32[9,1,2,2,128]{4,3,2,1,0:T(2,128)S(1)}, f32[9,1,2,2,128]{4,3,2,1,0:T(2,128)S(1)}, u32[]{:S(2)}, u32[]{:S(2)}) collective-permute-start(f32[9,1,2,2,128]{4,3,2,1,0:T(2,128)S(1)} %get-tuple-element.424), channel_id=1, source_target_pairs={{32,0},{64,32},{96,64},{128,96},{160,128},{192,160},{224,192},{256... | collective-permute-start | bytes 55304 | tf_op jit(solution)/shard_map/ppermute | solution.py:22
  15.6 12.2 %collective-permute-start.2 = (f32[9,4,1,2,128]{4,3,2,1,0:T(2,128)S(1)}, f32[9,4,1,2,128]{4,3,2,1,0:T(2,128)S(1)}, u32[]{:S(2)}, u32[]{:S(2)}) collective-permute-start(f32[9,4,1,2,128]{4,3,2,1,0:T(2,128)S(1)} %get-tuple-element.403), channel_id=1, source_target_pairs={{0,4},{4,8},{8,12},{12,16},{16,20},{20,24},{24,28},{28,0},{1,5},{5... | collective-permute-start | bytes 110600 | tf_op jit(solution)/shard_map/ppermute | solution.py:20
  25.8 9.6 %collective-permute-start.3 = (f32[9,4,1,2,128]{4,3,2,1,0:T(2,128)S(1)}, f32[9,4,1,2,128]{4,3,2,1,0:T(2,128)S(1)}, u32[]{:S(2)}, u32[]{:S(2)}) collective-permute-start(f32[9,4,1,2,128]{4,3,2,1,0:T(2,128)S(1)} %get-tuple-element.404), channel_id=1, source_target_pairs={{4,0},{8,4},{12,8},{16,12},{20,16},{24,20},{28,24},{0,28},{5,1},{9... | collective-permute-start | bytes 110600 | tf_op jit(solution)/shard_map/ppermute | solution.py:22
  35.6 6.9 %collective-permute-start.4 = (f32[9,4,4,1,128]{4,3,2,1,0:T(1,128)S(1)}, f32[9,4,4,1,128]{4,3,2,1,0:T(1,128)S(1)}, u32[]{:S(2)}, u32[]{:S(2)}) collective-permute-start(f32[9,4,4,1,128]{4,3,2,1,0:T(1,128)S(1)} %get-tuple-element.351), channel_id=1, source_target_pairs={{0,1},{1,2},{2,3},{3,0},{4,5},{5,6},{6,7},{7,4},{8,9},{9,10},{10,1... | collective-permute-start | bytes 221192 | tf_op jit(solution)/shard_map/ppermute | solution.py:20
  38.8 5.1 %collective-permute-start.5 = (f32[9,4,4,1,128]{4,3,2,1,0:T(1,128)S(1)}, f32[9,4,4,1,128]{4,3,2,1,0:T(1,128)S(1)}, u32[]{:S(2)}, u32[]{:S(2)}) collective-permute-start(f32[9,4,4,1,128]{4,3,2,1,0:T(1,128)S(1)} %get-tuple-element.352), channel_id=1, source_target_pairs={{1,0},{2,1},{3,2},{0,3},{5,4},{6,5},{7,6},{4,7},{9,8},{10,9},{11,1... | collective-permute-start | bytes 221192 | tf_op jit(solution)/shard_map/ppermute | solution.py:22
  61.3 0.7 copy-start.5
  61.3 0.7 copy-start.4
  62.1 70.2 %copy-start = (f32[2,2,2,128]{3,2,1,0:T(2,128)}, f32[2,2,2,128]{3,2,1,0:T(2,128)S(1)}, u32[]{:S(2)}) copy-start(f32[2,2,2,128]{3,2,1,0:T(2,128)S(1)} %get-tuple-element.185) | copy-start | bytes 12292
  62.1 10.6 %collective-permute-start.6 = (f32[1,1,2,2,128]{4,3,2,1,0:T(2,128)S(1)}, f32[1,1,2,2,128]{4,3,2,1,0:T(2,128)S(1)}, u32[]{:S(2)}, u32[]{:S(2)}) collective-permute-start(f32[1,1,2,2,128]{4,3,2,1,0:T(2,128)S(1)} %get-tuple-element.521), channel_id=1, source_target_pairs={{0,32},{32,64},{64,96},{96,128},{128,160},{160,192},{192,224},{224... | collective-permute-start | bytes 6152 | tf_op jit(solution)/shard_map/ppermute | solution.py:20
  64.0 9.3 %collective-permute-start.7 = (f32[1,1,2,2,128]{4,3,2,1,0:T(2,128)S(1)}, f32[1,1,2,2,128]{4,3,2,1,0:T(2,128)S(1)}, u32[]{:S(2)}, u32[]{:S(2)}) collective-permute-start(f32[1,1,2,2,128]{4,3,2,1,0:T(2,128)S(1)} %get-tuple-element.522), channel_id=1, source_target_pairs={{32,0},{64,32},{96,64},{128,96},{160,128},{192,160},{224,192},{256... | collective-permute-start | bytes 6152 | tf_op jit(solution)/shard_map/ppermute | solution.py:22
  73.4 5.0 %collective-permute-start.8 = (f32[1,4,1,2,128]{4,3,2,1,0:T(2,128)S(1)}, f32[1,4,1,2,128]{4,3,2,1,0:T(2,128)S(1)}, u32[]{:S(2)}, u32[]{:S(2)}) collective-permute-start(f32[1,4,1,2,128]{4,3,2,1,0:T(2,128)S(1)} %get-tuple-element.515), channel_id=1, source_target_pairs={{0,4},{4,8},{8,12},{12,16},{16,20},{20,24},{24,28},{28,0},{1,5},{5... | collective-permute-start | bytes 12296 | tf_op jit(solution)/shard_map/ppermute | solution.py:20
  76.4 8.8 %collective-permute-start.9 = (f32[1,4,1,2,128]{4,3,2,1,0:T(2,128)S(1)}, f32[1,4,1,2,128]{4,3,2,1,0:T(2,128)S(1)}, u32[]{:S(2)}, u32[]{:S(2)}) collective-permute-start(f32[1,4,1,2,128]{4,3,2,1,0:T(2,128)S(1)} %get-tuple-element.516), channel_id=1, source_target_pairs={{4,0},{8,4},{12,8},{16,12},{20,16},{24,20},{28,24},{0,28},{5,1},{9... | collective-permute-start | bytes 12296 | tf_op jit(solution)/shard_map/ppermute | solution.py:22
  85.3 6.5 %collective-permute-start.10 = (f32[1,4,4,1,128]{4,3,2,1,0:T(1,128)S(1)}, f32[1,4,4,1,128]{4,3,2,1,0:T(1,128)S(1)}, u32[]{:S(2)}, u32[]{:S(2)}) collective-permute-start(f32[1,4,4,1,128]{4,3,2,1,0:T(1,128)S(1)} %get-tuple-element.499), channel_id=1, source_target_pairs={{0,1},{1,2},{2,3},{3,0},{4,5},{5,6},{6,7},{7,4},{8,9},{9,10},{10,1... | collective-permute-start | bytes 24584 | tf_op jit(solution)/shard_map/ppermute | solution.py:20
  88.5 4.4 %collective-permute-start.11 = (f32[1,4,4,1,128]{4,3,2,1,0:T(1,128)S(1)}, f32[1,4,4,1,128]{4,3,2,1,0:T(1,128)S(1)}, u32[]{:S(2)}, u32[]{:S(2)}) collective-permute-start(f32[1,4,4,1,128]{4,3,2,1,0:T(1,128)S(1)} %get-tuple-element.500), channel_id=1, source_target_pairs={{1,0},{2,1},{3,2},{0,3},{5,4},{6,5},{7,6},{4,7},{9,8},{10,9},{11,1... | collective-permute-start | bytes 24584 | tf_op jit(solution)/shard_map/ppermute | solution.py:22
where the time goes:
time: 140 us
  other arithmetic  64 us (46%)
  starting transfers between devices  51.9 us (37%)
  waiting for transfers between devices  18.5 us (13%)
  local copies, waits for them, and re-layouts  4.02 us (3%)
    reduce_sum x8, other arithmetic, force_block(): jnp.sum(weight * parts[axis_id], axis=-1)  45.5 us
    ppermute x6, starting transfers between devices, extended(): lax.ppermute(tail, axis, [(i, (i + 1) % count) for i in range(count)])  25.9 us
    ppermute x6, starting transfers between devices, extended(): lax.ppermute(head, axis, [((i + 1) % count, i) for i in range(count)])  25.9 us
    ppermute x6, waiting for transfers between devices, extended(): lax.ppermute(head, axis, [((i + 1) % count, i) for i in range(count)])  18.5 us
    reduce_sum x9, other arithmetic, density_block(): total = total + jnp.sum(neighbour[7][..., None, :] * value, axis=-1)  16.8 us
    unnamed x20, local copies, waits for them, and re-layouts  3.48 us
  transfers between devices with their start and end apart: 12, of which 6 were waited for; matrix products, arithmetic and copies ran while one was open for 0% of the time, Pallas kernels for 0%

commit v1 on v0

v1 whole, which is shorter than its diff:
```python
import functools
import math

import jax
import jax.numpy as jnp
from jax import lax
from jax.experimental import pallas as pl
from jax.experimental.pallas import tpu as pltpu
from jax.sharding import PartitionSpec as P

MESH = pl.DeviceIdType.MESH
AXES = ("gx", "gy", "gz")
KERNEL_NORM = 21.0 / (2.0 * math.pi)
F32 = jnp.float32
LANES = 128
VMEM_BYTES = 24 * 1024 * 1024

AROUND = sorted(
    (
        (a, b, c)
        for a in (-1, 0, 1)
        for b in (-1, 0, 1)
        for c in (-1, 0, 1)
        if (a, b, c) != (0, 0, 0)
    ),
    key=lambda d: (-abs(d[1]), -abs(d[0]), -abs(d[2]), d),
)
STEPS = [16 * a + 4 * b + c for a in (-1, 0, 1) for b in (-1, 0, 1) for c in (-1, 0, 1)]


def device_at(step, sizes):
    return tuple(
        lax.rem(lax.axis_index(axis) + (move + size), size) if move else lax.axis_index(axis)
        for axis, move, size in zip(AXES, step, sizes)
    )


def leaving(step):
    return tuple({0: pl.ds(1, 2), 1: pl.ds(2, 1), -1: pl.ds(1, 1)}[move] for move in step)


def arriving(step):
    return tuple({0: pl.ds(1, 2), 1: pl.ds(0, 1), -1: pl.ds(3, 1)}[move] for move in step)


def greet(sizes):
    barrier = pltpu.get_barrier_semaphore()
    for step in AROUND:
        pl.semaphore_signal(
            barrier, inc=1, device_id=device_at(step, sizes), device_id_type=MESH
        )


def exchange(cells, sizes, send_sem, recv_sem):
    pl.semaphore_wait(pltpu.get_barrier_semaphore(), len(AROUND))
    copies = []
    for index, step in enumerate(AROUND):
        copy = pltpu.make_async_remote_copy(
            src_ref=cells.at[leaving(step)],
            dst_ref=cells.at[arriving(step)],
            send_sem=send_sem.at[index],
            recv_sem=recv_sem.at[index],
            device_id=device_at(step, sizes),
            device_id_type=MESH,
        )
        copy.start()
        copies.append(copy)
    for copy in copies:
        copy.wait()


def fields_kernel(sizes, offsets, velocities, smoothing, mass, cells, send_sem, recv_sem):
    greet(sizes)
    for c in range(8):
        x, y, z = 1 + c // 4, 1 + (c // 2) % 2, 1 + c % 2
        rows = [offsets[8 * d + c : 8 * d + c + 1] for d in range(3)]
        rows += [mass[c : c + 1]]
        rows += [velocities[8 * d + c : 8 * d + c + 1] for d in range(3)]
        rows += [smoothing[c : c + 1]]
        for row, value in enumerate(rows):
            cells[x, y, z, row : row + 1, :] = value
    exchange(cells, sizes, send_sem, recv_sem)


def density_exchange_kernel(sizes, density, factor, cells, send_sem, recv_sem):
    greet(sizes)
    for c in range(8):
        x, y, z = 1 + c // 4, 1 + (c // 2) % 2, 1 + c % 2
        cells[x, y, z, 0:1, :] = density[c : c + 1]
        cells[x, y, z, 1:2, :] = factor[c : c + 1]
    exchange(cells, sizes, send_sem, recv_sem)


def wide(row):
    return jnp.broadcast_to(row, (8, LANES))


def corner(c):
    return (
        lax.convert_element_type(c // 16, F32),
        lax.convert_element_type((c // 4) % 4, F32),
        lax.convert_element_type(c % 4, F32),
    )


def own_cell(c):
    return 16 * (1 + c // 4) + 4 * (1 + (c // 2) % 2) + 1 + c % 2


def rank_active(active, ranks, counts):
    live = active[...] == 1
    flags = jnp.where(live, 1.0, 0.0).astype(F32)
    ahead = lax.broadcasted_iota(jnp.int32, (LANES, LANES), 0) < lax.broadcasted_iota(
        jnp.int32, (LANES, LANES), 1
    )
    before = jnp.dot(
        flags.astype(jnp.bfloat16),
        jnp.where(ahead, 1.0, 0.0).astype(jnp.bfloat16),
        preferred_element_type=F32,
    )
    ranks[...] = jnp.where(live, before, -1.0)
    for c in range(8):
        counts[c] = jnp.sum(flags[c : c + 1]).astype(jnp.int32)


def chosen(ranks, c, group):
    places = lax.broadcasted_iota(jnp.int32, (8, LANES), 0) + 8 * group
    return wide(ranks[pl.ds(c, 1), :]) == places.astype(F32)


def pick(mask, row):
    return jnp.sum(jnp.where(mask, row, 0.0), axis=1, keepdims=True)


def density_kernel(cells, active, entropy, prior, density, factor, spread, ranks, counts):
    rank_active(active, ranks, counts)

    def prepare(c, carry):
        px, py, pz = corner(c)
        spread[4 * c] = wide(4.0 * (cells[c, 0:1, :] + px))
        spread[4 * c + 1] = wide(4.0 * (cells[c, 1:2, :] + py))
        spread[4 * c + 2] = wide(4.0 * (cells[c, 2:3, :] + pz))
        spread[4 * c + 3] = wide(cells[c, 3:4, :])
        return carry

    lax.fori_loop(0, 64, prepare, 0, unroll=4)

    def cell(c, carry):
        here = own_cell(c)

        def group_step(group, total):
            mask = chosen(ranks, c, group)
            xi = wide_lanes(pick(mask, spread[4 * here]))
            yi = wide_lanes(pick(mask, spread[4 * here + 1]))
            zi = wide_lanes(pick(mask, spread[4 * here + 2]))
            hi = wide_lanes(pick(mask, wide(cells[here, 7:8, :])))
            hi4 = 4.0 * hi
            acc = jnp.zeros((8, LANES), F32)
            for step in STEPS:
                j = 4 * (here + step)
                dx = xi - spread[j]
                dy = yi - spread[j + 1]
                dz = zi - spread[j + 2]
                sq = dx * dx + dy * dy + dz * dz
                r4 = sq * lax.rsqrt(jnp.maximum(sq, 1e-30))
                u = jnp.maximum(hi4 - r4, 0.0)
                u2 = u * u
                acc = acc + (u2 * u2) * ((hi + r4) * spread[j + 3])
            h2 = hi * hi
            h4 = h2 * h2
            value = jnp.sum(acc, axis=1, keepdims=True) * ((KERNEL_NORM / 256.0) / (h4 * h4))
            return total + jnp.where(mask, value, 0.0)

        total = lax.fori_loop(
            0, (counts[c] + 7) // 8, group_step, jnp.zeros((8, LANES), F32)
        )
        density[pl.ds(c, 1), :] = jnp.sum(total, axis=0, keepdims=True)
        return carry

    lax.fori_loop(0, 8, cell, 0)
    value = jnp.where(active[...] == 1, density[...], prior[...])
    density[...] = value
    factor[...] = entropy[...] * jnp.exp(jnp.log(value) * (-1.0 / 3.0))


def wide_lanes(column):
    return jnp.broadcast_to(column, (8, LANES))


FIELDS = 13


def strength(h):
    h2 = h * h
    h4 = h2 * h2
    return (2.5 * KERNEL_NORM) / (h4 * h4)


def force_kernel(cells, states, active, accel, spread, ranks, counts):
    rank_active(active, ranks, counts)

    def prepare(c, carry):
        px, py, pz = corner(c)
        at = FIELDS * c
        tile = cells[c]
        mass, h = tile[3:4], tile[7:8]
        rho = states[c, 0:1, :]
        fac = states[c, 1:2, :]
        rows = [tile[0:1] + px, tile[1:2] + py, tile[2:3] + pz]
        rows += [40.0 * tile[4:5], 40.0 * tile[5:6], 40.0 * tile[6:7]]
        rows += [h, 0.05 * h, mass * strength(h), mass]
        rows += [rho, 8.0 * fac, jnp.sqrt((5.0 / 3.0) * fac * rho)]
        for k, row in enumerate(rows):
            spread[at + k] = wide(row)
        return carry

    lax.fori_loop(0, 64, prepare, 0, unroll=2)

    def cell(c, carry):
        here = own_cell(c)

        def group_step(group, totals):
            mask = chosen(ranks, c, group)
            own = [
                wide_lanes(pick(mask, spread[FIELDS * here + k]))
                for k in (0, 1, 2, 3, 4, 5, 6, 7, 10, 11, 12)
            ]
            xi, yi, zi, ui_x, ui_y, ui_z, hi, ei, rhoi, faci, soundi = own
            bi = strength(hi)
            ax = jnp.zeros((8, LANES), F32)
            ay = jnp.zeros((8, LANES), F32)
            az = jnp.zeros((8, LANES), F32)
            for step in STEPS:
                j = FIELDS * (here + step)
                dx = xi - spread[j]
                dy = yi - spread[j + 1]
                dz = zi - spread[j + 2]
                sq = dx * dx + dy * dy + dz * dz
                app = (
                    dx * (ui_x - spread[j + 3])
                    + dy * (ui_y - spread[j + 4])
                    + dz * (ui_z - spread[j + 5])
                )
                r = sq * lax.rsqrt(jnp.maximum(sq, 1e-30))
                near = jnp.maximum(hi - r, 0.0)
                far = jnp.maximum(spread[j + 6] - r, 0.0)
                e = ei + spread[j + 7]
                m = e * jnp.minimum(app, 0.0) / (sq + e * e)
                visc = m * (m - (soundi + spread[j + 12])) / (rhoi + spread[j + 10])
                g_near = (near * near) * (near * (bi * spread[j + 9]))
                g_far = (far * far) * (far * spread[j + 8])
                w = (faci + visc) * g_near + (spread[j + 11] + visc) * g_far
                ax = ax + w * dx
                ay = ay + w * dy
                az = az + w * dz
            return tuple(
                total + jnp.where(mask, jnp.sum(a, axis=1, keepdims=True), 0.0)
                for total, a in zip(totals, (ax, ay, az))
            )

        zero = jnp.zeros((8, LANES), F32)
        totals = lax.fori_loop(0, (counts[c] + 7) // 8, group_step, (zero, zero, zero))
        for d in range(3):
            accel[pl.ds(8 * d + c, 1), :] = jnp.sum(totals[d], axis=0, keepdims=True)
        return carry

    lax.fori_loop(0, 8, cell, 0)


def vmem(count):
    return [pl.BlockSpec(memory_space=pltpu.VMEM)] * count


def remote_call(kernel, rows, count, collective_id):
    return pl.pallas_call(
        kernel,
        out_shape=jax.ShapeDtypeStruct((4, 4, 4, rows, LANES), F32),
        in_specs=vmem(count),
        out_specs=vmem(1)[0],
        scratch_shapes=[
            pltpu.SemaphoreType.DMA((len(AROUND),)),
            pltpu.SemaphoreType.DMA((len(AROUND),)),
        ],
        compiler_params=pltpu.CompilerParams(
            collective_id=collective_id, has_side_effects=True, vmem_limit_bytes=VMEM_BYTES
        ),
    )


def body(sizes, offsets, velocities, smoothing, mass, entropy, prior_density, active):
    flat = lambda a: a.reshape(-1, LANES)
    offsets, velocities = flat(offsets), flat(velocities)
    smoothing, mass, entropy = flat(smoothing), flat(mass), flat(entropy)
    prior_density, active = flat(prior_density), flat(active)
    cells = remote_call(functools.partial(fields_kernel, sizes), 8, 4, 0)(
        offsets, velocities, smoothing, mass
    ).reshape(64, 8, LANES)
    own = jax.ShapeDtypeStruct((8, LANES), F32)
    density, factor = pl.pallas_call(
        density_kernel,
        out_shape=(own, own),
        in_specs=vmem(4),
        out_specs=tuple(vmem(2)),
        scratch_shapes=[
            pltpu.VMEM((4 * 64, 8, LANES), F32),
            pltpu.VMEM((8, LANES), F32),
            pltpu.SMEM((8,), jnp.int32),
        ],
        compiler_params=pltpu.CompilerParams(vmem_limit_bytes=VMEM_BYTES),
    )(cells, active, entropy, prior_density)
    states = remote_call(functools.partial(density_exchange_kernel, sizes), 2, 2, 1)(
        density, factor
    ).reshape(64, 2, LANES)
    accel = pl.pallas_call(
        force_kernel,
        out_shape=jax.ShapeDtypeStruct((24, LANES), F32),
        in_specs=vmem(3),
        out_specs=vmem(1)[0],
        scratch_shapes=[
            pltpu.VMEM((FIELDS * 64, 8, LANES), F32),
            pltpu.VMEM((8, LANES), F32),
            pltpu.SMEM((8,), jnp.int32),
        ],
        compiler_params=pltpu.CompilerParams(vmem_limit_bytes=VMEM_BYTES),
    )(cells, states, active)
    return density.reshape(2, 2, 2, LANES), accel.reshape(3, 2, 2, 2, LANES)


def solution(mesh):
    sizes = tuple(mesh.shape[axis] for axis in AXES)
    spec = P("gx", "gy", "gz", None)
    spec3 = P(None, "gx", "gy", "gz", None)
    return jax.shard_map(
        functools.partial(body, sizes),
        mesh=mesh,
        in_specs=(spec3, spec3, spec, spec, spec, spec, spec),
        out_specs=(spec, spec3),
        check_vma=False,
    )
```

time: 140 us -> 80.1 us (0.57)
  Pallas kernels: 0 us -> 75.6 us
  other arithmetic: 64 us -> 0 us
  starting transfers between devices: 51.9 us -> 0 us
  waiting for transfers between devices: 18.5 us -> 0 us
    pallas_call x0 -> x4, Pallas kernels: none -> 75.6 us  [the longest x1 23.4 us: body(): remote_call(functools.partial(fields_kernel, sizes), 8, 4, 0)]
    reduce_sum x17 -> x0, other arithmetic: 62.3 us -> none  [the longest x8 45.5 us: force_block(): jnp.sum(weight * parts[axis_id], axis=-1)]
    ppermute x12 -> x0, starting transfers between devices: 51.9 us -> none  [the longest x6 25.9 us: extended(): lax.ppermute(tail, axis, [(i, (i + 1) % count) for i in range(count)])]
    ppermute x12 -> x0, waiting for transfers between devices: 18.5 us -> none  [the longest x6 18.5 us: extended(): lax.ppermute(head, axis, [((i + 1) % count, i) for i in range(count)])]
    unnamed x20 -> x16, local copies, waits for them, and re-layouts: 3.48 us -> 3.48 us
  transfers between devices with their start and end apart: 12 -> 0, of which waited for: 6 -> 0; matrix products, arithmetic and copies ran while one was open for 0% -> 0% of each run, Pallas kernels for 0% -> 0%
where the time goes in v1:
time: 80.1 us; the launch traced here: 79.8 us
  Pallas kernels  75.6 us (94%)
  local copies, waits for them, and re-layouts  3.48 us (4%)
    pallas_call x1, Pallas kernels, body(): remote_call(functools.partial(fields_kernel, sizes), 8, 4, 0)  23.4 us
    pallas_call x1, Pallas kernels, body(): pl.pallas_call(force_kernel, out_shape=jax.ShapeDtypeStruct((24, LANES),...  22.4 us
    pallas_call x1, Pallas kernels, body(): remote_call(functools.partial(density_exchange_kernel, sizes), 2, 2, 1)  15.1 us
    pallas_call x1, Pallas kernels, body(): pl.pallas_call(density_kernel, out_shape=(own, own), in_specs=vmem(4), ou...  14.7 us
    unnamed x16, local copies, waits for them, and re-layouts  3.48 us

profile of v1, /device:TPU:1, one launch (start us, length us, event | category | flops | bytes accessed | tf_op | source)
XLA Modules:
  0.0 79.8 jit_solution(10446697684815028597)
XLA Ops:
  0.6 0.0 copy-start.1
  0.6 0.7 copy-done.1
  1.3 0.0 copy-start.2
  1.3 0.7 copy-done.2
  2.0 0.0 copy-start.3
  2.0 0.7 copy-done.3
  2.7 0.0 copy-start.4
  2.7 0.7 copy-done.4
  3.4 0.0 copy-start
  3.4 0.0 copy-start.5
  3.4 0.0 copy-start.6
  3.4 23.4 %shard_map.86 = f32[4,4,4,8,128]{4,3,2,1,0:T(8,128)S(1)} custom-call(f32[24,128]{1,0:T(8,128)S(1)} %bitcast.16, f32[24,128]{1,0:T(8,128)S(1)} %bitcast.17, f32[8,128]{1,0:T(8,128)S(1)} %bitcast.18, f32[8,128]{1,0:T(8,128)S(1)} %bitcast.19), custom_call_target="tpu_custom_call" | custom-call | tf_op jit(solution)/shard_map/pallas_call | solution.py:295
  26.8 0.0 copy-done
  26.8 0.0 copy-done.5
  26.9 0.0 copy-done.6
  26.9 14.7 %shard_map.87 = (f32[8,128]{1,0:T(8,128)}, f32[8,128]{1,0:T(8,128)S(1)}) custom-call(f32[64,8,128]{2,1,0:T(8,128)S(1)} %bitcast.11, s32[8,128]{1,0:T(8,128)S(1)} %bitcast.14, f32[8,128]{1,0:T(8,128)S(1)} %bitcast.20, f32[8,128]{1,0:T(8,128)S(1)} %bitcast.21), custom_call_target="tpu_custom_call" | custom-call | tf_op jit(solution)/shard_map/pallas_call | solution.py:299
  41.6 0.0 copy-start.7
  41.6 0.7 copy-done.7
  42.2 15.1 %shard_map.88 = f32[4,4,4,2,128]{4,3,2,1,0:T(2,128)S(1)} custom-call(f32[8,128]{1,0:T(8,128)S(1)} %copy-done.7, f32[8,128]{1,0:T(8,128)S(1)} %get-tuple-element.5.factor), custom_call_target="tpu_custom_call" | custom-call | tf_op jit(solution)/shard_map/pallas_call | solution.py:311
  57.4 22.4 %shard_map.89 = f32[24,128]{1,0:T(8,128)} custom-call(f32[64,8,128]{2,1,0:T(8,128)S(1)} %bitcast.12, f32[64,2,128]{2,1,0:T(2,128)S(1)} %bitcast.13, s32[8,128]{1,0:T(8,128)S(1)} %bitcast.15), custom_call_target="tpu_custom_call" | custom-call | tf_op jit(solution)/shard_map/pallas_call | solution.py:314
Async XLA Ops:
  0.6 0.7 copy-start.1
  1.3 0.7 copy-start.2
  2.0 0.7 copy-start.3
  2.7 0.7 copy-start.4
  3.4 23.4 %copy-start = (s32[2,2,2,128]{3,2,1,0:T(2,128)S(1)}, s32[2,2,2,128]{3,2,1,0:T(2,128)}, u32[]{:S(2)}) copy-start(s32[2,2,2,128]{3,2,1,0:T(2,128)} %param.13) | copy-start | bytes 12292
  3.4 23.4 %copy-start.5 = (f32[2,2,2,128]{3,2,1,0:T(2,128)S(1)}, f32[2,2,2,128]{3,2,1,0:T(2,128)}, u32[]{:S(2)}) copy-start(f32[2,2,2,128]{3,2,1,0:T(2,128)} %param.11) | copy-start | bytes 12292
  3.4 23.4 %copy-start.6 = (f32[2,2,2,128]{3,2,1,0:T(2,128)S(1)}, f32[2,2,2,128]{3,2,1,0:T(2,128)}, u32[]{:S(2)}) copy-start(f32[2,2,2,128]{3,2,1,0:T(2,128)} %param.12) | copy-start | bytes 12292
  41.6 0.7 copy-start.7

commit v2 on v0

v2 whole, which is shorter than its diff:
```python
import functools
import math

import jax
import jax.numpy as jnp
from jax import lax
from jax.experimental import pallas as pl
from jax.experimental.pallas import tpu as pltpu
from jax.sharding import PartitionSpec as P

MESH = pl.DeviceIdType.MESH
AXES = ("gx", "gy", "gz")
KERNEL_NORM = 21.0 / (2.0 * math.pi)
F32 = jnp.float32
LANES = 128
VMEM_BYTES = 30 * 1024 * 1024

AROUND = sorted(
    (
        (a, b, c)
        for a in (-1, 0, 1)
        for b in (-1, 0, 1)
        for c in (-1, 0, 1)
        if (a, b, c) != (0, 0, 0)
    ),
    key=lambda d: (-abs(d[1]), -abs(d[0]), -abs(d[2]), d),
)
COUNT = len(AROUND)
JX, JY, JZ, JM, JU, JV, JW, JH, JE, JB = range(10)
J_TILES = 10
JR, JF, JS = range(3)
S_TILES = 3
IX, IY, IZ, IH, IU, IV, IW, IE, IB, IR, IF, IS = range(12)
I_TILES = 12
GROUPS = 16
OWN = [(x, y, z) for x in (1, 2) for y in (1, 2) for z in (1, 2)]
GHOST = [
    (x, y, z)
    for x in range(4)
    for y in range(4)
    for z in range(4)
    if not (x in (1, 2) and y in (1, 2) and z in (1, 2))
]


def device_at(step, sizes):
    return tuple(
        lax.rem(lax.axis_index(axis) + (move + size), size) if move else lax.axis_index(axis)
        for axis, move, size in zip(AXES, step, sizes)
    )


def leaving(step):
    return tuple({0: pl.ds(1, 2), 1: pl.ds(2, 1), -1: pl.ds(1, 1)}[move] for move in step)


def arriving(step):
    return tuple({0: pl.ds(1, 2), 1: pl.ds(0, 1), -1: pl.ds(3, 1)}[move] for move in step)


def send_all(cells, sizes, send_sem, recv_sem):
    copies = {}
    for index, step in enumerate(AROUND):
        copies[step] = pltpu.make_async_remote_copy(
            src_ref=cells.at[leaving(step)],
            dst_ref=cells.at[arriving(step)],
            send_sem=send_sem.at[index],
            recv_sem=recv_sem.at[index],
            device_id=device_at(step, sizes),
            device_id_type=MESH,
        )
        copies[step].start()
    return copies


def flat(x, y, z):
    return 16 * x + 4 * y + z


def wide(row):
    return jnp.broadcast_to(row, (8, LANES))


def strength(h4):
    h2 = h4 * h4
    q = h2 * h2
    return (2.5 * KERNEL_NORM * 1024.0) / (q * q)


def ranks_of(active, order):
    live = active == 1
    before = jnp.dot(
        jnp.where(live, 1.0, 0.0).astype(jnp.bfloat16),
        order.astype(jnp.bfloat16),
        preferred_element_type=F32,
    )
    return jnp.where(live, before, -1.0)


def order_kernel(order):
    ahead = lax.broadcasted_iota(jnp.int32, (LANES, LANES), 0) < lax.broadcasted_iota(
        jnp.int32, (LANES, LANES), 1
    )
    order[...] = jnp.where(ahead, 1.0, 0.0)


def chosen(ranks, c, group):
    places = lax.broadcasted_iota(jnp.int32, (8, LANES), 0) + 8 * group
    return wide(ranks[pl.ds(c, 1), :]) == places.astype(F32)


def across(tile):
    return jnp.broadcast_to(jnp.sum(tile, axis=1, keepdims=True), (8, LANES))


def density_sum(own, spread, sites, acc):
    x, y, z, h4 = own
    h = 0.25 * h4
    for site in sites:
        j = J_TILES * site
        dx = x - spread[j + JX]
        dy = y - spread[j + JY]
        dz = z - spread[j + JZ]
        sq = dx * dx + dy * dy + dz * dz
        r4 = sq * lax.rsqrt(jnp.maximum(sq, 1e-30))
        u = jnp.maximum(h4 - r4, 0.0)
        u2 = u * u
        acc = acc + (u2 * u2) * ((h + r4) * spread[j + JM])
    return acc


def force_sum(own, spread, states, sites, acc):
    x, y, z, h4, vx, vy, vz, e4, b, rho, fac, sound = own
    ax, ay, az = acc
    for site in sites:
        j = J_TILES * site
        s = S_TILES * site
        dx = x - spread[j + JX]
        dy = y - spread[j + JY]
        dz = z - spread[j + JZ]
        sq = dx * dx + dy * dy + dz * dz
        app = dx * (vx - spread[j + JU]) + dy * (vy - spread[j + JV]) + dz * (vz - spread[j + JW])
        r4 = sq * lax.rsqrt(jnp.maximum(sq, 1e-30))
        near = jnp.maximum(h4 - r4, 0.0)
        far = jnp.maximum(spread[j + JH] - r4, 0.0)
        e = e4 + spread[j + JE]
        m = e * jnp.minimum(app, 0.0) / (sq + e * e)
        visc = m * (m - (sound + states[s + JS])) / (rho + states[s + JR])
        g_near = (near * near) * (near * (b * spread[j + JM]))
        g_far = (far * far) * (far * spread[j + JB])
        w = (fac + visc) * g_near + (states[s + JF] + visc) * g_far
        ax = ax + w * dx
        ay = ay + w * dy
        az = az + w * dz
    return ax, ay, az


def ghost_sites(c, which):
    gx, gy, gz = 3 * (c // 4), 3 * ((c // 2) % 2), 3 * (c % 2)
    z_side = [flat(x, y, gz) for x in (1, 2) for y in (1, 2)]
    x_side = [flat(gx, y, z) for y in (1, 2) for z in (1, 2, gz)]
    y_side = [flat(x, gy, z) for x in (1, 2, gx) for z in (1, 2, gz)]
    return {"z": z_side, "x": x_side, "y": y_side}[which]


def own_sites():
    return [flat(x, y, z) for x, y, z in OWN]


def place_tiles(cells, spread, x, y, z):
    at = J_TILES * flat(x, y, z)
    spread[at + JX] = wide(4.0 * (cells[x, y, z, 0:1, :] + float(x)))
    spread[at + JY] = wide(4.0 * (cells[x, y, z, 1:2, :] + float(y)))
    spread[at + JZ] = wide(4.0 * (cells[x, y, z, 2:3, :] + float(z)))
    spread[at + JM] = wide(cells[x, y, z, 3:4, :])


def motion_tiles(cells, spread, x, y, z):
    at = J_TILES * flat(x, y, z)
    tile = cells[x, y, z]
    h4 = 4.0 * tile[7:8]
    spread[at + JU] = wide(40.0 * tile[4:5])
    spread[at + JV] = wide(40.0 * tile[5:6])
    spread[at + JW] = wide(40.0 * tile[6:7])
    spread[at + JH] = wide(h4)
    spread[at + JE] = wide(0.05 * h4)
    spread[at + JB] = wide(tile[3:4] * strength(h4))


def state_tiles(rho, fac, states, site):
    at = S_TILES * site
    states[at + JR] = wide(rho)
    states[at + JF] = wide(8.0 * fac)
    states[at + JS] = wide(jnp.sqrt((5.0 / 3.0) * fac * rho))


def gather_kernel(
    sizes,
    order,
    offsets,
    velocities,
    smoothing,
    mass,
    entropy,
    prior,
    active,
    spread,
    particles,
    partial,
    gas,
    ranks,
    density,
    cells,
    own_states,
    sums,
    send_sem,
    recv_sem,
    send2_sem,
    recv2_sem,
):
    barrier = pltpu.get_barrier_semaphore()
    for step in AROUND:
        pl.semaphore_signal(
            barrier, inc=1, device_id=device_at(step, sizes), device_id_type=MESH
        )
    for c, (x, y, z) in enumerate(OWN):
        rows = [offsets[8 * d + c : 8 * d + c + 1] for d in range(3)]
        rows += [mass[c : c + 1]]
        rows += [velocities[8 * d + c : 8 * d + c + 1] for d in range(3)]
        rows += [smoothing[c : c + 1]]
        for row, value in enumerate(rows):
            cells[x, y, z, row : row + 1, :] = value
    pl.semaphore_wait(barrier, COUNT)
    copies = send_all(cells, sizes, send_sem, recv_sem)

    for x, y, z in OWN:
        place_tiles(cells, spread, x, y, z)
        motion_tiles(cells, spread, x, y, z)
    ranks[...] = ranks_of(active[...], order[...])

    def pick(t, carry):
        c, group = t // GROUPS, t % GROUPS
        here = J_TILES * flat(1 + c // 4, 1 + (c // 2) % 2, 1 + c % 2)
        mask = chosen(ranks, c, group)
        at = I_TILES * t
        for i_tile, j_tile in (
            (IX, JX),
            (IY, JY),
            (IZ, JZ),
            (IU, JU),
            (IV, JV),
            (IW, JW),
        ):
            particles[at + i_tile] = across(jnp.where(mask, spread[here + j_tile], 0.0))
        h4 = across(jnp.where(mask, spread[here + JH], 0.0))
        particles[at + IH] = h4
        particles[at + IE] = 0.05 * h4
        particles[at + IB] = strength(h4)
        particles[at + IF] = across(jnp.where(mask, wide(entropy[pl.ds(c, 1), :]), 0.0))
        return carry

    lax.fori_loop(0, 8 * GROUPS, pick, 0, unroll=2)

    def density_inputs(t):
        at = I_TILES * t
        return [particles[at + k] for k in (IX, IY, IZ, IH)]

    def inner_density(t, carry):
        sums[t] = density_sum(
            density_inputs(t), spread, own_sites(), jnp.zeros((8, LANES), F32)
        )
        return carry

    lax.fori_loop(0, 8 * GROUPS, inner_density, 0, unroll=2)

    for which in ("z", "x", "y"):
        axis = {"z": 2, "x": 0, "y": 1}[which]
        later = {"z": (0, 1), "x": (1,), "y": ()}[which]
        for step in AROUND:
            if step[axis] and not any(step[k] for k in later):
                copies[step].wait_recv()
        for x, y, z in GHOST:
            cell = (x, y, z)
            if cell[axis] in (0, 3) and not any(cell[k] in (0, 3) for k in later):
                place_tiles(cells, spread, x, y, z)

        def outer_density(t, carry, which=which):
            sums[t] = density_sum(
                density_inputs(t), spread, ghost_sites(t // GROUPS, which), sums[t]
            )
            return carry

        lax.fori_loop(0, 8 * GROUPS, outer_density, 0, unroll=2)

    def settle(c, carry):
        total = jnp.zeros((8, LANES), F32)
        for group in range(GROUPS):
            t = GROUPS * c + group
            at = I_TILES * t
            mask = chosen(ranks, c, group)
            h4 = particles[at + IH]
            h2 = h4 * h4
            q = h2 * h2
            rho = across(sums[t]) * ((KERNEL_NORM * 256.0) / (q * q))
            total = total + jnp.where(mask, rho, 0.0)
            fac = particles[at + IF] * jnp.exp(jnp.log(rho) * (-1.0 / 3.0))
            particles[at + IR] = rho
            particles[at + IF] = 8.0 * fac
            particles[at + IS] = jnp.sqrt((5.0 / 3.0) * fac * rho)
        density[pl.ds(c, 1), :] = jnp.sum(total, axis=0, keepdims=True)
        return carry

    lax.fori_loop(0, 8, settle, 0)
    rho = jnp.where(active[...] == 1, density[...], prior[...])
    density[...] = rho
    fac = entropy[...] * jnp.exp(jnp.log(rho) * (-1.0 / 3.0))
    for c, (x, y, z) in enumerate(OWN):
        gas[x, y, z, 0:1, :] = rho[c : c + 1]
        gas[x, y, z, 1:2, :] = fac[c : c + 1]
    copies2 = send_all(gas, sizes, send2_sem, recv2_sem)

    for c, (x, y, z) in enumerate(OWN):
        state_tiles(rho[c : c + 1], fac[c : c + 1], own_states, flat(x, y, z))

    def inner_force(t, carry):
        at = I_TILES * t
        zero = jnp.zeros((8, LANES), F32)
        acc = force_sum(
            [particles[at + k] for k in range(I_TILES)],
            spread,
            own_states,
            own_sites(),
            (zero, zero, zero),
        )
        for d in range(3):
            partial[3 * t + d] = acc[d]
        return carry

    lax.fori_loop(0, 8 * GROUPS, inner_force, 0)
    for x, y, z in GHOST:
        motion_tiles(cells, spread, x, y, z)
    for step in AROUND:
        copies[step].wait_send()
        copies2[step].wait()


def force_kernel(
    spread, particles, partial, gas, ranks, density_in, density, accel, states, sums, counts
):
    density[...] = density_in[...]
    last = jnp.max(ranks[...], axis=1, keepdims=True)
    for c in range(8):
        counts[c] = (jnp.max(last[c : c + 1]) + 1.0).astype(jnp.int32)

    def prepare(site, carry):
        state_tiles(gas[site, 0:1, :], gas[site, 1:2, :], states, site)
        return carry

    lax.fori_loop(0, 64, prepare, 0, unroll=4)

    def cell(c, carry):
        groups = (counts[c] + 7) // 8
        sites = [site for which in ("z", "x", "y") for site in ghost_sites(c, which)]

        def group_step(group, inner):
            t = GROUPS * c + group
            at = I_TILES * t
            acc = force_sum(
                [particles[at + k] for k in range(I_TILES)],
                spread,
                states,
                sites,
                tuple(partial[3 * t + d] for d in range(3)),
            )
            for d in range(3):
                sums[3 * group + d] = acc[d]
            return inner

        lax.fori_loop(0, groups, group_step, 0)

        def fold(quad, totals):
            for k in range(4):
                group = 4 * quad + k
                mask = chosen(ranks, c, group)
                totals = tuple(
                    total + jnp.where(mask, across(sums[3 * group + d]), 0.0)
                    for d, total in enumerate(totals)
                )
            return totals

        zero = jnp.zeros((8, LANES), F32)
        totals = lax.fori_loop(0, (groups + 3) // 4, fold, (zero, zero, zero))
        for d in range(3):
            accel[pl.ds(8 * d + c, 1), :] = 0.25 * jnp.sum(totals[d], axis=0, keepdims=True)
        return carry

    lax.fori_loop(0, 8, cell, 0)


def vmem(count):
    return [pl.BlockSpec(memory_space=pltpu.VMEM)] * count


def tiles(count):
    return jax.ShapeDtypeStruct((count, 8, LANES), F32)


def body(sizes, *args):
    rows = [a.reshape(-1, LANES) for a in args]
    cell_rows = jax.ShapeDtypeStruct((8, LANES), F32)
    order = pl.pallas_call(
        order_kernel,
        out_shape=jax.ShapeDtypeStruct((LANES, LANES), F32),
        out_specs=vmem(1)[0],
        compiler_params=pltpu.CompilerParams(vmem_limit_bytes=VMEM_BYTES),
        cost_estimate=pl.CostEstimate(flops=10_000_000, bytes_accessed=8_000_000, transcendentals=0),
    )()
    spread, particles, partial, gas, ranks, density = pl.pallas_call(
        functools.partial(gather_kernel, sizes),
        out_shape=(
            tiles(64 * J_TILES),
            tiles(8 * GROUPS * I_TILES),
            tiles(8 * GROUPS * 3),
            jax.ShapeDtypeStruct((4, 4, 4, 2, LANES), F32),
            cell_rows,
            cell_rows,
        ),
        in_specs=vmem(8),
        out_specs=tuple(vmem(6)),
        scratch_shapes=[
            pltpu.VMEM((4, 4, 4, 8, LANES), F32),
            pltpu.VMEM((64 * S_TILES, 8, LANES), F32),
            pltpu.VMEM((8 * GROUPS, 8, LANES), F32),
            pltpu.SemaphoreType.DMA((COUNT,)),
            pltpu.SemaphoreType.DMA((COUNT,)),
            pltpu.SemaphoreType.DMA((COUNT,)),
            pltpu.SemaphoreType.DMA((COUNT,)),
        ],
        compiler_params=pltpu.CompilerParams(
            collective_id=0, has_side_effects=True, vmem_limit_bytes=VMEM_BYTES
        ),
    )(order, *rows)
    density, accel = pl.pallas_call(
        force_kernel,
        out_shape=(cell_rows, jax.ShapeDtypeStruct((24, LANES), F32)),
        in_specs=vmem(6),
        out_specs=tuple(vmem(2)),
        scratch_shapes=[
            pltpu.VMEM((64 * S_TILES, 8, LANES), F32),
            pltpu.VMEM((GROUPS * 3, 8, LANES), F32),
            pltpu.SMEM((8,), jnp.int32),
        ],
        compiler_params=pltpu.CompilerParams(vmem_limit_bytes=VMEM_BYTES),
    )(spread, particles, partial, gas.reshape(64, 2, LANES), ranks, density)
    return density.reshape(2, 2, 2, LANES), accel.reshape(3, 2, 2, 2, LANES)


def solution(mesh):
    sizes = tuple(mesh.shape[axis] for axis in AXES)
    spec = P("gx", "gy", "gz", None)
    spec3 = P(None, "gx", "gy", "gz", None)
    return jax.shard_map(
        functools.partial(body, sizes),
        mesh=mesh,
        in_specs=(spec3, spec3, spec, spec, spec, spec, spec),
        out_specs=(spec, spec3),
        check_vma=False,
    )
```

time: 140 us -> 65.8 us (0.47)
  the two profiles are of different devices: /device:TPU:1 before, /device:TPU:129 now
where the time goes in v2:
time: 65.8 us; the launch traced here: 65.4 us
  Pallas kernels  59.9 us (91%)
  local copies, waits for them, and re-layouts  4.84 us (7%)
  between operations  0.66 us (1%)
    pallas_call x1, Pallas kernels, body(): pl.pallas_call(functools.partial(gather_kernel, sizes), out_shape=(tiles(...  48.6 us
    pallas_call x1, Pallas kernels, body(): pl.pallas_call(force_kernel, out_shape=(cell_rows, jax.ShapeDtypeStruct((...  11.3 us
    unnamed x14, local copies, waits for them, and re-layouts  4.84 us

profile of v2, /device:TPU:129, one launch (start us, length us, event | category | flops | bytes accessed | tf_op | source)
XLA Modules:
  0.0 65.4 jit_solution(774833156360461696)
XLA Ops:
  0.6 0.0 copy-start
  0.7 0.7 %copy-done = f32[3,2,2,2,128]{4,3,2,1,0:T(2,128)S(1)} copy-done((f32[3,2,2,2,128]{4,3,2,1,0:T(2,128)S(1)}, f32[3,2,2,2,128]{4,3,2,1,0:T(2,128)}, u32[]{:S(2)}) %copy-start) | copy-done | bytes 12312
  1.4 0.0 copy-start.1
  1.4 0.7 %copy-done.1 = f32[3,2,2,2,128]{4,3,2,1,0:T(2,128)S(1)} copy-done((f32[3,2,2,2,128]{4,3,2,1,0:T(2,128)S(1)}, f32[3,2,2,2,128]{4,3,2,1,0:T(2,128)}, u32[]{:S(2)}) %copy-start.1) | copy-done | bytes 12312
  2.1 0.0 copy-start.2
  2.1 0.7 %copy-done.2 = f32[2,2,2,128]{3,2,1,0:T(2,128)S(1)} copy-done((f32[2,2,2,128]{3,2,1,0:T(2,128)S(1)}, f32[2,2,2,128]{3,2,1,0:T(2,128)}, u32[]{:S(2)}) %copy-start.2) | copy-done | bytes 4120
  2.8 0.0 copy-start.3
  2.8 0.7 %copy-done.3 = f32[2,2,2,128]{3,2,1,0:T(2,128)S(1)} copy-done((f32[2,2,2,128]{3,2,1,0:T(2,128)S(1)}, f32[2,2,2,128]{3,2,1,0:T(2,128)}, u32[]{:S(2)}) %copy-start.3) | copy-done | bytes 4120
  3.4 0.0 copy-start.4
  3.4 0.7 %copy-done.4 = f32[2,2,2,128]{3,2,1,0:T(2,128)S(1)} copy-done((f32[2,2,2,128]{3,2,1,0:T(2,128)S(1)}, f32[2,2,2,128]{3,2,1,0:T(2,128)}, u32[]{:S(2)}) %copy-start.4) | copy-done | bytes 4120
  4.1 0.0 copy-start.5
  4.1 0.7 %copy-done.5 = f32[2,2,2,128]{3,2,1,0:T(2,128)S(1)} copy-done((f32[2,2,2,128]{3,2,1,0:T(2,128)S(1)}, f32[2,2,2,128]{3,2,1,0:T(2,128)}, u32[]{:S(2)}) %copy-start.5) | copy-done | bytes 4120
  4.8 0.0 copy-start.6
  4.8 0.7 %copy-done.6 = s32[2,2,2,128]{3,2,1,0:T(2,128)S(1)} copy-done((s32[2,2,2,128]{3,2,1,0:T(2,128)S(1)}, s32[2,2,2,128]{3,2,1,0:T(2,128)}, u32[]{:S(2)}) %copy-start.6) | copy-done | bytes 4120
  5.5 48.6 %shard_map.87 = (f32[640,8,128]{2,1,0:T(8,128)S(1)}, f32[1536,8,128]{2,1,0:T(8,128)S(1)}, f32[384,8,128]{2,1,0:T(8,128)S(1)}, f32[4,4,4,2,128]{4,3,2,1,0:T(2,128...) custom-call(f32[128,128]{1,0:T(8,128)S(1)} %shard_map.86.order, f32[24,128]{1,0:T(8,128)S(1)} %bitcast.11, ...), custom_call_target="tpu_custom_call" | custom-call | tf_op jit(solution)/shard_map/pallas_call | solution.py:418
  54.1 11.3 %shard_map.88 = (f32[8,128]{1,0:T(8,128)}, f32[24,128]{1,0:T(8,128)}) custom-call(f32[640,8,128]{2,1,0:T(8,128)S(1)} %get-tuple-element.10.spread, f32[1536,8,128]{2,1,0:T(8,128)S(1)} %get-tuple-element.11.particles, f32[384,8,128]{2,1,0:T(8,128)S(1)} %get-tuple-element.12.partial, f32[64,2,128]{2,1,0:T(2,128)S(1)} %bitcast.10, ...), custom_call_target="tpu_custom_call" | custom-call | tf_op jit(solution)/shard_map/pallas_call | solution.py:443
  (1 shorter events, 0.0 us)
Async XLA Ops:
  0.6 0.7 %copy-start = (f32[3,2,2,2,128]{4,3,2,1,0:T(2,128)S(1)}, f32[3,2,2,2,128]{4,3,2,1,0:T(2,128)}, u32[]{:S(2)}) copy-start(f32[3,2,2,2,128]{4,3,2,1,0:T(2,128)} %param.7) | copy-start | bytes 36868
  1.4 0.7 %copy-start.1 = (f32[3,2,2,2,128]{4,3,2,1,0:T(2,128)S(1)}, f32[3,2,2,2,128]{4,3,2,1,0:T(2,128)}, u32[]{:S(2)}) copy-start(f32[3,2,2,2,128]{4,3,2,1,0:T(2,128)} %param.8) | copy-start | bytes 36868
  2.1 0.7 %copy-start.2 = (f32[2,2,2,128]{3,2,1,0:T(2,128)S(1)}, f32[2,2,2,128]{3,2,1,0:T(2,128)}, u32[]{:S(2)}) copy-start(f32[2,2,2,128]{3,2,1,0:T(2,128)} %param.9) | copy-start | bytes 12292
  2.8 0.7 %copy-start.3 = (f32[2,2,2,128]{3,2,1,0:T(2,128)S(1)}, f32[2,2,2,128]{3,2,1,0:T(2,128)}, u32[]{:S(2)}) copy-start(f32[2,2,2,128]{3,2,1,0:T(2,128)} %param.10) | copy-start | bytes 12292
  3.4 0.7 %copy-start.4 = (f32[2,2,2,128]{3,2,1,0:T(2,128)S(1)}, f32[2,2,2,128]{3,2,1,0:T(2,128)}, u32[]{:S(2)}) copy-start(f32[2,2,2,128]{3,2,1,0:T(2,128)} %param.11) | copy-start | bytes 12292
  4.1 0.7 %copy-start.5 = (f32[2,2,2,128]{3,2,1,0:T(2,128)S(1)}, f32[2,2,2,128]{3,2,1,0:T(2,128)}, u32[]{:S(2)}) copy-start(f32[2,2,2,128]{3,2,1,0:T(2,128)} %param.12) | copy-start | bytes 12292
  4.8 0.7 %copy-start.6 = (s32[2,2,2,128]{3,2,1,0:T(2,128)S(1)}, s32[2,2,2,128]{3,2,1,0:T(2,128)}, u32[]{:S(2)}) copy-start(s32[2,2,2,128]{3,2,1,0:T(2,128)} %param.13) | copy-start | bytes 12292

commit v3 on v2

--- a/solution.py
+++ b/solution.py
@@ -87,23 +87,19 @@
     return (2.5 * KERNEL_NORM * 1024.0) / (q * q)
 
 
-def ranks_of(active, order):
+def ranks_of(active):
     live = active == 1
+    ahead = lax.broadcasted_iota(jnp.int32, (LANES, LANES), 0) < lax.broadcasted_iota(
+        jnp.int32, (LANES, LANES), 1
+    )
     before = jnp.dot(
         jnp.where(live, 1.0, 0.0).astype(jnp.bfloat16),
-        order.astype(jnp.bfloat16),
+        jnp.where(ahead, 1.0, 0.0).astype(jnp.bfloat16),
         preferred_element_type=F32,
     )
     return jnp.where(live, before, -1.0)
 
 
-def order_kernel(order):
-    ahead = lax.broadcasted_iota(jnp.int32, (LANES, LANES), 0) < lax.broadcasted_iota(
-        jnp.int32, (LANES, LANES), 1
-    )
-    order[...] = jnp.where(ahead, 1.0, 0.0)
-
-
 def chosen(ranks, c, group):
     places = lax.broadcasted_iota(jnp.int32, (8, LANES), 0) + 8 * group
     return wide(ranks[pl.ds(c, 1), :]) == places.astype(F32)
@@ -113,20 +109,21 @@
     return jnp.broadcast_to(jnp.sum(tile, axis=1, keepdims=True), (8, LANES))
 
 
-def density_sum(own, spread, sites, acc):
-    x, y, z, h4 = own
-    h = 0.25 * h4
+def density_sum(owns, spread, sites, accs):
+    accs = list(accs)
     for site in sites:
         j = J_TILES * site
-        dx = x - spread[j + JX]
-        dy = y - spread[j + JY]
-        dz = z - spread[j + JZ]
-        sq = dx * dx + dy * dy + dz * dz
-        r4 = sq * lax.rsqrt(jnp.maximum(sq, 1e-30))
-        u = jnp.maximum(h4 - r4, 0.0)
-        u2 = u * u
-        acc = acc + (u2 * u2) * ((h + r4) * spread[j + JM])
-    return acc
+        xj, yj, zj, mj = (spread[j + k] for k in (JX, JY, JZ, JM))
+        for k, (x, y, z, h4) in enumerate(owns):
+            dx = x - xj
+            dy = y - yj
+            dz = z - zj
+            sq = dx * dx + dy * dy + dz * dz
+            r4 = sq * lax.rsqrt(jnp.maximum(sq, 1e-30))
+            u = jnp.maximum(h4 - r4, 0.0)
+            u2 = u * u
+            accs[k] = accs[k] + (u2 * u2) * ((0.25 * h4 + r4) * mj)
+    return accs
 
 
 def force_sum(own, spread, states, sites, acc):
@@ -196,7 +193,19 @@
 
 def gather_kernel(
     sizes,
-    order,
+    offsets_in,
+    velocities_in,
+    smoothing_in,
+    mass_in,
+    entropy_in,
+    prior_in,
+    active_in,
+    spread,
+    particles,
+    partial,
+    gas,
+    ranks,
+    density,
     offsets,
     velocities,
     smoothing,
@@ -204,15 +213,11 @@
     entropy,
     prior,
     active,
-    spread,
-    particles,
-    partial,
-    gas,
-    ranks,
-    density,
     cells,
     own_states,
     sums,
+    picked,
+    load_sem,
     send_sem,
     recv_sem,
     send2_sem,
@@ -223,6 +228,25 @@
         pl.semaphore_signal(
             barrier, inc=1, device_id=device_at(step, sizes), device_id_type=MESH
         )
+    loads = [
+        pltpu.make_async_copy(source, target, load_sem.at[index])
+        for index, (source, target) in enumerate(
+            (
+                (offsets_in, offsets),
+                (velocities_in, velocities),
+                (smoothing_in, smoothing),
+                (mass_in, mass),
+                (entropy_in, entropy),
+                (prior_in, prior),
+                (active_in, active),
+            )
+        )
+    ]
+    for load in loads:
+        load.start()
+    for load in loads:
+        load.wait()
+
     for c, (x, y, z) in enumerate(OWN):
         rows = [offsets[8 * d + c : 8 * d + c + 1] for d in range(3)]
         rows += [mass[c : c + 1]]
@@ -236,42 +260,49 @@
     for x, y, z in OWN:
         place_tiles(cells, spread, x, y, z)
         motion_tiles(cells, spread, x, y, z)
-    ranks[...] = ranks_of(active[...], order[...])
-
-    def pick(t, carry):
-        c, group = t // GROUPS, t % GROUPS
-        here = J_TILES * flat(1 + c // 4, 1 + (c // 2) % 2, 1 + c % 2)
-        mask = chosen(ranks, c, group)
-        at = I_TILES * t
-        for i_tile, j_tile in (
-            (IX, JX),
-            (IY, JY),
-            (IZ, JZ),
-            (IU, JU),
-            (IV, JV),
-            (IW, JW),
-        ):
-            particles[at + i_tile] = across(jnp.where(mask, spread[here + j_tile], 0.0))
-        h4 = across(jnp.where(mask, spread[here + JH], 0.0))
-        particles[at + IH] = h4
-        particles[at + IE] = 0.05 * h4
-        particles[at + IB] = strength(h4)
-        particles[at + IF] = across(jnp.where(mask, wide(entropy[pl.ds(c, 1), :]), 0.0))
-        return carry
-
-    lax.fori_loop(0, 8 * GROUPS, pick, 0, unroll=2)
+    ranks[...] = ranks_of(active[...])
+
+    for c, (x, y, z) in enumerate(OWN):
+        tile = cells[x, y, z]
+        h4 = 4.0 * tile[7:8]
+        picked[0:1, :] = 4.0 * (tile[0:1] + float(x))
+        picked[1:2, :] = 4.0 * (tile[1:2] + float(y))
+        picked[2:3, :] = 4.0 * (tile[2:3] + float(z))
+        picked[3:4, :] = h4
+        picked[4:7, :] = 40.0 * tile[4:7]
+        picked[7:8, :] = 0.05 * h4
+        picked[8:9, :] = strength(h4)
+        picked[9:10, :] = entropy[c : c + 1]
+        picked[10:16, :] = jnp.zeros((6, LANES), F32)
+        places = lax.broadcasted_iota(jnp.int32, (LANES, LANES), 0).astype(F32)
+        found = places == jnp.broadcast_to(ranks[c : c + 1], (LANES, LANES))
+        columns = lax.dot_general(
+            jnp.where(found, 1.0, 0.0),
+            picked[...],
+            (((1,), (1,)), ((), ())),
+            precision=lax.Precision.HIGHEST,
+            preferred_element_type=F32,
+        )
+        for group in range(GROUPS):
+            at = I_TILES * (GROUPS * c + group)
+            for source, target in enumerate((IX, IY, IZ, IH, IU, IV, IW, IE, IB, IF)):
+                particles[at + target] = jnp.broadcast_to(
+                    columns[8 * group : 8 * group + 8, source : source + 1], (8, LANES)
+                )
 
     def density_inputs(t):
         at = I_TILES * t
         return [particles[at + k] for k in (IX, IY, IZ, IH)]
 
-    def inner_density(t, carry):
-        sums[t] = density_sum(
-            density_inputs(t), spread, own_sites(), jnp.zeros((8, LANES), F32)
-        )
+    def inner_density(quad, carry):
+        zero = jnp.zeros((8, LANES), F32)
+        some = [4 * quad + k for k in range(4)]
+        accs = density_sum([density_inputs(t) for t in some], spread, own_sites(), [zero] * 4)
+        for t, acc in zip(some, accs):
+            sums[t] = acc
         return carry
 
-    lax.fori_loop(0, 8 * GROUPS, inner_density, 0, unroll=2)
+    lax.fori_loop(0, 2 * GROUPS, inner_density, 0)
 
     for which in ("z", "x", "y"):
         axis = {"z": 2, "x": 0, "y": 1}[which]
@@ -284,13 +315,19 @@
             if cell[axis] in (0, 3) and not any(cell[k] in (0, 3) for k in later):
                 place_tiles(cells, spread, x, y, z)
 
-        def outer_density(t, carry, which=which):
-            sums[t] = density_sum(
-                density_inputs(t), spread, ghost_sites(t // GROUPS, which), sums[t]
-            )
-            return carry
-
-        lax.fori_loop(0, 8 * GROUPS, outer_density, 0, unroll=2)
+        for c in range(8):
+            sites = ghost_sites(c, which)
+
+            def outer_density(quad, carry, c=c, sites=sites):
+                some = [GROUPS * c + 4 * quad + k for k in range(4)]
+                accs = density_sum(
+                    [density_inputs(t) for t in some], spread, sites, [sums[t] for t in some]
+                )
+                for t, acc in zip(some, accs):
+                    sums[t] = acc
+                return carry
+
+            lax.fori_loop(0, GROUPS // 4, outer_density, 0)
 
     def settle(c, carry):
         total = jnp.zeros((8, LANES), F32)
@@ -298,10 +335,7 @@
             t = GROUPS * c + group
             at = I_TILES * t
             mask = chosen(ranks, c, group)
-            h4 = particles[at + IH]
-            h2 = h4 * h4
-            q = h2 * h2
-            rho = across(sums[t]) * ((KERNEL_NORM * 256.0) / (q * q))
+            rho = across(sums[t]) * (0.1 * particles[at + IB])
             total = total + jnp.where(mask, rho, 0.0)
             fac = particles[at + IF] * jnp.exp(jnp.log(rho) * (-1.0 / 3.0))
             particles[at + IR] = rho
@@ -336,7 +370,7 @@
             partial[3 * t + d] = acc[d]
         return carry
 
-    lax.fori_loop(0, 8 * GROUPS, inner_force, 0)
+    lax.fori_loop(0, 8 * GROUPS, inner_force, 0, unroll=2)
     for x, y, z in GHOST:
         motion_tiles(cells, spread, x, y, z)
     for step in AROUND:
@@ -358,11 +392,12 @@
 
     lax.fori_loop(0, 64, prepare, 0, unroll=4)
 
-    def cell(c, carry):
+    zero = jnp.zeros((8, LANES), F32)
+    for c in range(8):
         groups = (counts[c] + 7) // 8
         sites = [site for which in ("z", "x", "y") for site in ghost_sites(c, which)]
 
-        def group_step(group, inner):
+        def group_step(group, inner, c=c, sites=sites):
             t = GROUPS * c + group
             at = I_TILES * t
             acc = force_sum(
@@ -378,7 +413,7 @@
 
         lax.fori_loop(0, groups, group_step, 0)
 
-        def fold(quad, totals):
+        def fold(quad, totals, c=c):
             for k in range(4):
                 group = 4 * quad + k
                 mask = chosen(ranks, c, group)
@@ -388,13 +423,9 @@
                 )
             return totals
 
-        zero = jnp.zeros((8, LANES), F32)
         totals = lax.fori_loop(0, (groups + 3) // 4, fold, (zero, zero, zero))
         for d in range(3):
-            accel[pl.ds(8 * d + c, 1), :] = 0.25 * jnp.sum(totals[d], axis=0, keepdims=True)
-        return carry
-
-    lax.fori_loop(0, 8, cell, 0)
+            accel[8 * d + c : 8 * d + c + 1, :] = 0.25 * jnp.sum(totals[d], axis=0, keepdims=True)
 
 
 def vmem(count):
@@ -406,15 +437,8 @@
 
 
 def body(sizes, *args):
-    rows = [a.reshape(-1, LANES) for a in args]
+    rows = [pltpu.with_memory_space_constraint(a.reshape(-1, LANES), pltpu.HBM) for a in args]
     cell_rows = jax.ShapeDtypeStruct((8, LANES), F32)
-    order = pl.pallas_call(
-        order_kernel,
-        out_shape=jax.ShapeDtypeStruct((LANES, LANES), F32),
-        out_specs=vmem(1)[0],
-        compiler_params=pltpu.CompilerParams(vmem_limit_bytes=VMEM_BYTES),
-        cost_estimate=pl.CostEstimate(flops=10_000_000, bytes_accessed=8_000_000, transcendentals=0),
-    )()
     spread, particles, partial, gas, ranks, density = pl.pallas_call(
         functools.partial(gather_kernel, sizes),
         out_shape=(
@@ -425,12 +449,21 @@
             cell_rows,
             cell_rows,
         ),
-        in_specs=vmem(8),
+        in_specs=[pl.BlockSpec(memory_space=pltpu.HBM)] * 7,
         out_specs=tuple(vmem(6)),
         scratch_shapes=[
+            pltpu.VMEM((24, LANES), F32),
+            pltpu.VMEM((24, LANES), F32),
+            pltpu.VMEM((8, LANES), F32),
+            pltpu.VMEM((8, LANES), F32),
+            pltpu.VMEM((8, LANES), F32),
+            pltpu.VMEM((8, LANES), F32),
+            pltpu.VMEM((8, LANES), jnp.int32),
             pltpu.VMEM((4, 4, 4, 8, LANES), F32),
             pltpu.VMEM((64 * S_TILES, 8, LANES), F32),
             pltpu.VMEM((8 * GROUPS, 8, LANES), F32),
+            pltpu.VMEM((16, LANES), F32),
+            pltpu.SemaphoreType.DMA((7,)),
             pltpu.SemaphoreType.DMA((COUNT,)),
             pltpu.SemaphoreType.DMA((COUNT,)),
             pltpu.SemaphoreType.DMA((COUNT,)),
@@ -439,7 +472,7 @@
         compiler_params=pltpu.CompilerParams(
             collective_id=0, has_side_effects=True, vmem_limit_bytes=VMEM_BYTES
         ),
-    )(order, *rows)
+    )(*rows)
     density, accel = pl.pallas_call(
         force_kernel,
         out_shape=(cell_rows, jax.ShapeDtypeStruct((24, LANES), F32)),

time: 65.8 us -> 52.5 us (0.80)
  the two profiles are of different devices: /device:TPU:129 before, /device:TPU:1 now
where the time goes in v3:
time: 52.5 us; the launch traced here: 52.3 us
  Pallas kernels  51.6 us (98%)
  between operations  0.64 us (1%)
    pallas_call x1, Pallas kernels, body(): pl.pallas_call(functools.partial(gather_kernel, sizes), out_shape=(tiles(...  41.8 us
    pallas_call x1, Pallas kernels, body(): pl.pallas_call(force_kernel, out_shape=(cell_rows, jax.ShapeDtypeStruct((...  9.9 us

profile of v3, /device:TPU:1, one launch (start us, length us, event | category | flops | bytes accessed | tf_op | source)
XLA Modules:
  0.0 52.3 jit_solution(9417431213152885831)
XLA Ops:
  0.6 41.8 %shard_map.86 = (f32[640,8,128]{2,1,0:T(8,128)S(1)}, f32[1536,8,128]{2,1,0:T(8,128)S(1)}, f32[384,8,128]{2,1,0:T(8,128)S(1)}, f32[4,4,4,2,128]{4,3,2,1,0:T(2,128...) custom-call(f32[24,128]{1,0:T(8,128)} %bitcast.11, f32[24,128]{1,0:T(8,128)} %bitcast.12, f32[8,128]{1,0:T(8,128)} %bitcast.13, ...), custom_call_target="tpu_custom_call" | custom-call | tf_op jit(solution)/shard_map/pallas_call | solution.py:442
  42.4 9.9 %shard_map.87 = (f32[8,128]{1,0:T(8,128)}, f32[24,128]{1,0:T(8,128)}) custom-call(f32[640,8,128]{2,1,0:T(8,128)S(1)} %get-tuple-element.10.spread, f32[1536,8,128]{2,1,0:T(8,128)S(1)} %get-tuple-element.11.particles, f32[384,8,128]{2,1,0:T(8,128)S(1)} %get-tuple-element.12.partial, f32[64,2,128]{2,1,0:T(2,128)S(1)} %bitcast.10, ...), custom_call_target="tpu_custom_call" | custom-call | tf_op jit(solution)/shard_map/pallas_call | solution.py:476

commit v4 on v3

v4 whole, which is shorter than its diff:
```python
import functools
import math

import jax
import jax.numpy as jnp
from jax import lax
from jax.experimental import pallas as pl
from jax.experimental.pallas import tpu as pltpu
from jax.sharding import PartitionSpec as P

MESH = pl.DeviceIdType.MESH
AXES = ("gx", "gy", "gz")
KERNEL_NORM = 21.0 / (2.0 * math.pi)
F32 = jnp.float32
LANES = 128
VMEM_BYTES = 18 * 1024 * 1024
BF16 = jnp.bfloat16
PARTS = 64

AROUND = sorted(
    (
        (a, b, c)
        for a in (-1, 0, 1)
        for b in (-1, 0, 1)
        for c in (-1, 0, 1)
        if (a, b, c) != (0, 0, 0)
    ),
    key=lambda d: (-abs(d[1]), -abs(d[0]), -abs(d[2]), d),
)
COUNT = len(AROUND)
JX, JY, JZ, JM, JH, JE, JB = range(7)
J_TILES = 7
JR, JF, JS = range(3)
S_TILES = 3
IX, IY, IZ, IH, IE, IB, IQ, IR, IF, IS = range(10)
I_TILES = 10
GROUPS = 16
OWN = [(x, y, z) for x in (1, 2) for y in (1, 2) for z in (1, 2)]
GHOST = [
    (x, y, z)
    for x in range(4)
    for y in range(4)
    for z in range(4)
    if not (x in (1, 2) and y in (1, 2) and z in (1, 2))
]


def device_at(step, sizes):
    return tuple(
        lax.rem(lax.axis_index(axis) + (move + size), size) if move else lax.axis_index(axis)
        for axis, move, size in zip(AXES, step, sizes)
    )


def leaving(step):
    return tuple({0: pl.ds(1, 2), 1: pl.ds(2, 1), -1: pl.ds(1, 1)}[move] for move in step)


def arriving(step):
    return tuple({0: pl.ds(1, 2), 1: pl.ds(0, 1), -1: pl.ds(3, 1)}[move] for move in step)


def send_all(cells, sizes, send_sem, recv_sem):
    copies = {}
    for index, step in enumerate(AROUND):
        copies[step] = pltpu.make_async_remote_copy(
            src_ref=cells.at[leaving(step)],
            dst_ref=cells.at[arriving(step)],
            send_sem=send_sem.at[index],
            recv_sem=recv_sem.at[index],
            device_id=device_at(step, sizes),
            device_id_type=MESH,
        )
        copies[step].start()
    return copies


def flat(x, y, z):
    return 16 * x + 4 * y + z


def wide(row):
    return jnp.broadcast_to(row, (8, LANES))


def strength(h4):
    h2 = h4 * h4
    q = h2 * h2
    return (2.5 * KERNEL_NORM * 1024.0) / (q * q)


def ranks_of(active):
    live = active == 1
    ahead = lax.broadcasted_iota(jnp.int32, (LANES, LANES), 0) < lax.broadcasted_iota(
        jnp.int32, (LANES, LANES), 1
    )
    before = jnp.dot(
        jnp.where(live, 1.0, 0.0).astype(jnp.bfloat16),
        jnp.where(ahead, 1.0, 0.0).astype(jnp.bfloat16),
        preferred_element_type=F32,
    )
    return jnp.where(live, before, -100.0)


def chosen(ranks, c, group):
    places = lax.broadcasted_iota(jnp.int32, (8, LANES), 0) + 8 * group
    return wide(ranks[pl.ds(c, 1), :]) == places.astype(F32)


def across(tile):
    return jnp.broadcast_to(jnp.sum(tile, axis=1, keepdims=True), (8, LANES))


def force_sum(own, spread, states, pairs, acc):
    x, y, z, h4, e4, b, _, rho, fac, sound = own
    ax, ay, az = acc
    for site, r4, app in pairs:
        j = J_TILES * site
        s = S_TILES * site
        near = jnp.maximum(h4 - r4, 0.0)
        far = jnp.maximum(spread[j + JH] - r4, 0.0)
        e = e4 + spread[j + JE]
        m = e * jnp.minimum(app, 0.0) / (r4 * r4 + e * e)
        visc = m * (m - (sound + states[s + JS])) / (rho + states[s + JR])
        g_near = (near * near) * (near * (b * spread[j + JM]))
        g_far = (far * far) * (far * spread[j + JB])
        w = (fac + visc) * g_near + (states[s + JF] + visc) * g_far
        ax = ax + w * (x - spread[j + JX])
        ay = ay + w * (y - spread[j + JY])
        az = az + w * (z - spread[j + JZ])
    return ax, ay, az


STAGES = {"z": (0, 4), "x": (32, 6), "y": (80, 9)}
PAIRS = 152


def own_site(k):
    return flat(1 + k // 4, 1 + (k // 2) % 2, 1 + k % 2)


def ghost_site(which, c, k):
    gx, gy, gz = 3 * (c // 4), 3 * ((c // 2) % 2), 3 * (c % 2)
    if which == "z":
        return flat(1 + k // 2, 1 + k % 2, gz)
    last = k % 3
    z = 1 + last + (last // 2) * (gz - 3)
    if which == "x":
        return flat(gx, 1 + k // 3, z)
    first = k // 3
    return flat(1 + first + (first // 2) * (gx - 3), gy, z)


def split(tile):
    one = tile.astype(BF16).astype(F32)
    two = (tile - one).astype(BF16).astype(F32)
    three = (tile - one - two).astype(BF16).astype(F32)
    return one, two, three


def stack(blocks):
    return jnp.concatenate(blocks, axis=0).astype(BF16)


def far_features(cells, features, right, x, y, z):
    site = flat(x, y, z)
    px = 4.0 * (cells[x, y, z, 0:1, :] + float(x - 2))
    py = 4.0 * (cells[x, y, z, 1:2, :] + float(y - 2))
    pz = 4.0 * (cells[x, y, z, 2:3, :] + float(z - 2))
    vx = 40.0 * cells[x, y, z, 3:4, :]
    vy = 40.0 * cells[x, y, z, 4:5, :]
    vz = 40.0 * cells[x, y, z, 5:6, :]
    rows = (px, py, pz, vx, vy, vz, px * px + py * py + pz * pz, px * vx + py * vy + pz * vz)
    for k, row in enumerate(rows):
        features[site, k : k + 1, :] = row
    one, two, three = split(features[site])
    index = lax.broadcasted_iota(jnp.int32, (8, LANES), 0)
    ones = jnp.where(index < 3, 1.0, 0.0)
    zero = jnp.zeros((8, LANES), F32)
    right[site, 0:16, :] = stack([one, one])
    right[site, 16:32, :] = stack([one, two])
    right[site, 32:48, :] = stack([two, three])
    right[site, 48:64, :] = stack([ones, zero])


def near_features(features, site):
    tile = features[site]
    px, py, pz, vx, vy, vz, square, dot = (tile[k : k + 1] for k in range(8))
    none = jnp.zeros((1, LANES), F32)
    one = jnp.ones((1, LANES), F32)
    zero = jnp.zeros((8, LANES), F32)
    result = []
    for rows, own in (
        ((-2.0 * px, -2.0 * py, -2.0 * pz, none, none, none, one, none), square),
        ((-vx, -vy, -vz, -px, -py, -pz, none, one), dot),
    ):
        u1, u2, u3 = split(jnp.concatenate(rows, axis=0))
        q = jnp.concatenate(list(split(own)) + [none] * 5, axis=0)
        result += [u1, u2, u3, u1, u2, u1, q, zero]
    return stack(result)


def place_tiles(cells, spread, x, y, z):
    at = J_TILES * flat(x, y, z)
    spread[at + JX] = wide(4.0 * (cells[x, y, z, 0:1, :] + float(x)))
    spread[at + JY] = wide(4.0 * (cells[x, y, z, 1:2, :] + float(y)))
    spread[at + JZ] = wide(4.0 * (cells[x, y, z, 2:3, :] + float(z)))
    h4 = 4.0 * cells[x, y, z, 7:8, :]
    spread[at + JH] = wide(h4)
    spread[at + JE] = wide(0.05 * h4)
    spread[at + JB] = wide(cells[x, y, z, 6:7, :] * strength(h4))


def mass_tile(cells, spread, x, y, z):
    spread[J_TILES * flat(x, y, z) + JM] = wide(cells[x, y, z, 6:7, :])


def state_tiles(rho, fac, states, site):
    at = S_TILES * site
    states[at + JR] = wide(rho)
    states[at + JF] = wide(8.0 * fac)
    states[at + JS] = wide(jnp.sqrt((5.0 / 3.0) * fac * rho))


def gather_kernel(
    sizes,
    offsets_in,
    velocities_in,
    smoothing_in,
    mass_in,
    entropy_in,
    prior_in,
    active_in,
    spread,
    particles,
    partial,
    gas,
    ranks,
    density,
    roots,
    approach,
    offsets,
    velocities,
    smoothing,
    mass,
    entropy,
    prior,
    active,
    cells,
    own_states,
    sums,
    picked,
    features,
    left,
    right,
    even,
    odd,
    own_roots,
    own_approach,
    load_sem,
    send_sem,
    recv_sem,
    send2_sem,
    recv2_sem,
):
    barrier = pltpu.get_barrier_semaphore()
    for step in AROUND:
        pl.semaphore_signal(
            barrier, inc=1, device_id=device_at(step, sizes), device_id_type=MESH
        )
    loads = [
        pltpu.make_async_copy(source, target, load_sem.at[index])
        for index, (source, target) in enumerate(
            (
                (offsets_in, offsets),
                (velocities_in, velocities),
                (smoothing_in, smoothing),
                (mass_in, mass),
                (entropy_in, entropy),
                (prior_in, prior),
                (active_in, active),
            )
        )
    ]
    for load in loads:
        load.start()
    for load in loads:
        load.wait()

    for c, (x, y, z) in enumerate(OWN):
        rows = [offsets[8 * d + c : 8 * d + c + 1] for d in range(3)]
        rows += [velocities[8 * d + c : 8 * d + c + 1] for d in range(3)]
        rows += [mass[c : c + 1], smoothing[c : c + 1]]
        for row, value in enumerate(rows):
            cells[x, y, z, row : row + 1, :] = value
    pl.semaphore_wait(barrier, COUNT)
    copies = send_all(cells, sizes, send_sem, recv_sem)

    for x, y, z in OWN:
        place_tiles(cells, spread, x, y, z)
        mass_tile(cells, spread, x, y, z)
        far_features(cells, features, right, x, y, z)
    ranks[...] = ranks_of(active[...])

    for c, (x, y, z) in enumerate(OWN):
        tile = cells[x, y, z]
        h4 = 4.0 * tile[7:8]
        picked[0:1, :] = 4.0 * (tile[0:1] + float(x))
        picked[1:2, :] = 4.0 * (tile[1:2] + float(y))
        picked[2:3, :] = 4.0 * (tile[2:3] + float(z))
        picked[3:4, :] = h4
        picked[4:5, :] = 0.05 * h4
        picked[5:6, :] = strength(h4)
        picked[6:7, :] = 0.25 * h4
        picked[7:8, :] = entropy[c : c + 1]
        places = lax.broadcasted_iota(jnp.int32, (LANES, LANES), 0).astype(F32)
        found = places == jnp.broadcast_to(ranks[c : c + 1], (LANES, LANES))
        found = jnp.where(found, 1.0, 0.0)
        near = lax.dot_general(
            found.astype(BF16),
            near_features(features, flat(x, y, z)),
            (((1,), (1,)), ((), ())),
            preferred_element_type=F32,
        )
        left[c, 0:LANES, :] = near[:, 0:PARTS].astype(BF16)
        left[c, LANES : 2 * LANES, :] = near[:, PARTS : 2 * PARTS].astype(BF16)
        columns = lax.dot_general(
            found,
            picked[...],
            (((1,), (1,)), ((), ())),
            precision=lax.Precision.HIGHEST,
            preferred_element_type=F32,
        )
        for group in range(GROUPS):
            at = I_TILES * (GROUPS * c + group)
            for source, target in enumerate((IX, IY, IZ, IH, IE, IB, IQ, IF)):
                particles[at + target] = jnp.broadcast_to(
                    columns[8 * group : 8 * group + 8, source : source + 1], (8, LANES)
                )

    def clear(t, carry):
        sums[t] = jnp.zeros((8, LANES), F32)
        return carry

    lax.fori_loop(0, 8 * GROUPS, clear, 0, unroll=8)

    def density_stage(per_cell, site_of, base, root_out, approach_out):
        total = 8 * per_cell

        def products(pair, target):
            c = pair // per_cell
            both = jnp.dot(
                left[c], right[site_of(c, pair % per_cell)], preferred_element_type=F32
            )
            target[...] = both[0:LANES]
            approach_out[base + pair] = both[LANES : 2 * LANES]

        def density_of(pair, source):
            c = pair // per_cell
            mass_j = spread[J_TILES * site_of(c, pair % per_cell) + JM]
            for group in range(GROUPS):
                t = GROUPS * c + group
                rows = slice(8 * group, 8 * group + 8)
                square = jnp.maximum(source[rows, :], 1e-12)
                r4 = square * lax.rsqrt(square)
                root_out[base + pair, rows, :] = r4
                u = jnp.maximum(particles[I_TILES * t + IH] - r4, 0.0)
                u2 = u * u
                sums[t] += (u2 * u2) * ((particles[I_TILES * t + IQ] + r4) * mass_j)

        products(0, even)

        def step(half, carry):
            products(2 * half + 1, odd)
            density_of(2 * half, even)
            products((2 * half + 2) % total, even)
            density_of(2 * half + 1, odd)
            return carry

        lax.fori_loop(0, total // 2, step, 0)

    density_stage(8, lambda c, k: own_site(k), 0, own_roots, own_approach)

    for which in ("z", "x", "y"):
        axis = {"z": 2, "x": 0, "y": 1}[which]
        later = {"z": (0, 1), "x": (1,), "y": ()}[which]
        for step in AROUND:
            if step[axis] and not any(step[k] for k in later):
                copies[step].wait_recv()
        for x, y, z in GHOST:
            cell = (x, y, z)
            if cell[axis] in (0, 3) and not any(cell[k] in (0, 3) for k in later):
                mass_tile(cells, spread, x, y, z)
                far_features(cells, features, right, x, y, z)
        base, per_cell = STAGES[which]
        density_stage(per_cell, functools.partial(ghost_site, which), base, roots, approach)

    for c in range(8):
        total = jnp.zeros((8, LANES), F32)
        for group in range(GROUPS):
            t = GROUPS * c + group
            rho = across(sums[t]) * (0.1 * particles[I_TILES * t + IB])
            particles[I_TILES * t + IR] = rho
            total = total + jnp.where(chosen(ranks, c, group), rho, 0.0)
        density[c : c + 1, :] = jnp.sum(total, axis=0, keepdims=True)
    rho = jnp.where(active[...] == 1, density[...], prior[...])
    density[...] = rho
    fac = entropy[...] * jnp.exp(jnp.log(rho) * (-1.0 / 3.0))
    for c, (x, y, z) in enumerate(OWN):
        gas[x, y, z, 0:1, :] = rho[c : c + 1]
        gas[x, y, z, 1:2, :] = fac[c : c + 1]
    copies2 = send_all(gas, sizes, send2_sem, recv2_sem)

    def settle(t, carry):
        at = I_TILES * t
        rho_i = particles[at + IR]
        fac_i = particles[at + IF] * jnp.exp(jnp.log(rho_i) * (-1.0 / 3.0))
        particles[at + IF] = 8.0 * fac_i
        particles[at + IS] = jnp.sqrt((5.0 / 3.0) * fac_i * rho_i)
        return carry

    lax.fori_loop(0, 8 * GROUPS, settle, 0, unroll=8)

    for c, (x, y, z) in enumerate(OWN):
        state_tiles(rho[c : c + 1], fac[c : c + 1], own_states, flat(x, y, z))

    def inner_force(t, carry):
        at = I_TILES * t
        rows = pl.ds(8 * (t % GROUPS), 8)
        zero = jnp.zeros((8, LANES), F32)
        acc = force_sum(
            [particles[at + k] for k in range(I_TILES)],
            spread,
            own_states,
            [
                (
                    own_site(k),
                    own_roots[8 * (t // GROUPS) + k, rows, :],
                    own_approach[8 * (t // GROUPS) + k, rows, :],
                )
                for k in range(8)
            ],
            (zero, zero, zero),
        )
        for d in range(3):
            partial[3 * t + d] = acc[d]
        return carry

    lax.fori_loop(0, 8 * GROUPS, inner_force, 0, unroll=2)
    for x, y, z in GHOST:
        place_tiles(cells, spread, x, y, z)
    for step in AROUND:
        copies[step].wait_send()
        copies2[step].wait()


def force_kernel(
    spread,
    particles,
    partial,
    gas,
    ranks,
    density_in,
    roots,
    approach,
    density,
    accel,
    states,
    sums,
    counts,
):
    density[...] = density_in[...]
    last = jnp.max(ranks[...], axis=1, keepdims=True)
    for c in range(8):
        counts[c] = (jnp.maximum(jnp.max(last[c : c + 1]), -1.0) + 8.0).astype(jnp.int32) // 8

    def prepare(site, carry):
        state_tiles(gas[site, 0:1, :], gas[site, 1:2, :], states, site)
        return carry

    lax.fori_loop(0, 64, prepare, 0, unroll=4)

    zero = jnp.zeros((8, LANES), F32)
    sums[...] = jnp.zeros(sums.shape, F32)

    def fold(c, group, totals):
        mask = chosen(ranks, c, group)
        at = 3 * (GROUPS * c + jnp.maximum(group, 0))
        return tuple(
            total + jnp.where(mask, across(sums[at + d]), 0.0) for d, total in enumerate(totals)
        )

    totals = []
    for c in range(8):
        pairs = [
            (ghost_site(which, c, k), base + per_cell * c + k)
            for which, (base, per_cell) in STAGES.items()
            for k in range(per_cell)
        ]

        def group_step(group, found, c=c, pairs=pairs):
            found = fold(c, group - 1, found)
            t = GROUPS * c + group
            rows = pl.ds(8 * group, 8)
            acc = force_sum(
                [particles[I_TILES * t + k] for k in range(I_TILES)],
                spread,
                states,
                [(site, roots[pair, rows, :], approach[pair, rows, :]) for site, pair in pairs],
                tuple(partial[3 * t + d] for d in range(3)),
            )
            for d in range(3):
                sums[3 * t + d] = acc[d]
            return found

        totals.append(lax.fori_loop(0, counts[c], group_step, (zero, zero, zero)))
    for c in range(8):
        found = fold(c, counts[c] - 1, totals[c])
        for d in range(3):
            accel[8 * d + c : 8 * d + c + 1, :] = 0.25 * jnp.sum(found[d], axis=0, keepdims=True)


def vmem(count):
    return [pl.BlockSpec(memory_space=pltpu.VMEM)] * count


def tiles(count):
    return jax.ShapeDtypeStruct((count, 8, LANES), F32)


def body(sizes, *args):
    rows = [pltpu.with_memory_space_constraint(a.reshape(-1, LANES), pltpu.HBM) for a in args]
    cell_rows = jax.ShapeDtypeStruct((8, LANES), F32)
    spread, particles, partial, gas, ranks, density, roots, approach = pl.pallas_call(
        functools.partial(gather_kernel, sizes),
        out_shape=(
            tiles(64 * J_TILES),
            tiles(8 * GROUPS * I_TILES),
            tiles(8 * GROUPS * 3),
            jax.ShapeDtypeStruct((4, 4, 4, 2, LANES), F32),
            cell_rows,
            cell_rows,
            jax.ShapeDtypeStruct((PAIRS, LANES, LANES), F32),
            jax.ShapeDtypeStruct((PAIRS, LANES, LANES), F32),
        ),
        in_specs=[pl.BlockSpec(memory_space=pltpu.HBM)] * 7,
        out_specs=tuple(vmem(8)),
        scratch_shapes=[
            pltpu.VMEM((24, LANES), F32),
            pltpu.VMEM((24, LANES), F32),
            pltpu.VMEM((8, LANES), F32),
            pltpu.VMEM((8, LANES), F32),
            pltpu.VMEM((8, LANES), F32),
            pltpu.VMEM((8, LANES), F32),
            pltpu.VMEM((8, LANES), jnp.int32),
            pltpu.VMEM((4, 4, 4, 8, LANES), F32),
            pltpu.VMEM((64 * S_TILES, 8, LANES), F32),
            pltpu.VMEM((8 * GROUPS, 8, LANES), F32),
            pltpu.VMEM((8, LANES), F32),
            pltpu.VMEM((64, 8, LANES), F32),
            pltpu.VMEM((8, 2 * LANES, PARTS), BF16),
            pltpu.VMEM((64, PARTS, LANES), BF16),
            pltpu.VMEM((LANES, LANES), F32),
            pltpu.VMEM((LANES, LANES), F32),
            pltpu.VMEM((64, LANES, LANES), F32),
            pltpu.VMEM((64, LANES, LANES), F32),
            pltpu.SemaphoreType.DMA((7,)),
            pltpu.SemaphoreType.DMA((COUNT,)),
            pltpu.SemaphoreType.DMA((COUNT,)),
            pltpu.SemaphoreType.DMA((COUNT,)),
            pltpu.SemaphoreType.DMA((COUNT,)),
        ],
        compiler_params=pltpu.CompilerParams(
            collective_id=0, has_side_effects=True, vmem_limit_bytes=VMEM_BYTES
        ),
    )(*rows)
    density, accel = pl.pallas_call(
        force_kernel,
        out_shape=(cell_rows, jax.ShapeDtypeStruct((24, LANES), F32)),
        in_specs=vmem(8),
        out_specs=tuple(vmem(2)),
        scratch_shapes=[
            pltpu.VMEM((64 * S_TILES, 8, LANES), F32),
            pltpu.VMEM((8 * GROUPS * 3, 8, LANES), F32),
            pltpu.SMEM((8,), jnp.int32),
        ],
        compiler_params=pltpu.CompilerParams(vmem_limit_bytes=VMEM_BYTES),
    )(spread, particles, partial, gas.reshape(64, 2, LANES), ranks, density, roots, approach)
    return density.reshape(2, 2, 2, LANES), accel.reshape(3, 2, 2, 2, LANES)


def solution(mesh):
    sizes = tuple(mesh.shape[axis] for axis in AXES)
    spec = P("gx", "gy", "gz", None)
    spec3 = P(None, "gx", "gy", "gz", None)
    return jax.shard_map(
        functools.partial(body, sizes),
        mesh=mesh,
        in_specs=(spec3, spec3, spec, spec, spec, spec, spec),
        out_specs=(spec, spec3),
        check_vma=False,
    )
```

time: 52.5 us -> 59.3 us (1.13)
  the two profiles are of different devices: /device:TPU:1 before, /device:TPU:7 now
where the time goes in v4:
time: 59.3 us; the launch traced here: 59.1 us
  Pallas kernels  58.5 us (99%)
  between operations  0.64 us (1%)
    pallas_call x1, Pallas kernels, body(): pl.pallas_call(functools.partial(gather_kernel, sizes), out_shape=(tiles(...  50.9 us
    pallas_call x1, Pallas kernels, body(): pl.pallas_call(force_kernel, out_shape=(cell_rows, jax.ShapeDtypeStruct((...  7.61 us

profile of v4, /device:TPU:7, one launch (start us, length us, event | category | flops | bytes accessed | tf_op | source)
XLA Modules:
  0.0 59.1 jit_solution(5608947659731860896)
XLA Ops:
  0.6 50.9 %shard_map.86 = (f32[448,8,128]{2,1,0:T(8,128)S(1)}, f32[1280,8,128]{2,1,0:T(8,128)S(1)}, f32[384,8,128]{2,1,0:T(8,128)S(1)}, f32[4,4,4,2,128]{4,3,2,1,0:T(2,128...) custom-call(f32[24,128]{1,0:T(8,128)} %bitcast.11, ...), custom_call_target="tpu_custom_call" | custom-call | tf_op jit(solution)/shard_map/pallas_call | solution.py:534
  51.5 7.6 %shard_map.87 = (f32[8,128]{1,0:T(8,128)}, f32[24,128]{1,0:T(8,128)}) custom-call(f32[448,8,128]{2,1,0:T(8,128)S(1)} %get-tuple-element.12.spread, f32[1280,8,128]{2,1,0:T(8,128)S(1)} %get-tuple-element.13.particles, f32[384,8,128]{2,1,0:T(8,128)S(1)} %get-tuple-element.14.partial, f32[64,2,128]{2,1,0:T(2,128)S(1)} %bitcast.10, ...), custom_call_target="tpu_custom_call" | custom-call | tf_op jit(solution)/shard_map/pallas_call | solution.py:577

commit v5 on v3

--- a/solution.py
+++ b/solution.py
@@ -13,7 +13,7 @@
 KERNEL_NORM = 21.0 / (2.0 * math.pi)
 F32 = jnp.float32
 LANES = 128
-VMEM_BYTES = 30 * 1024 * 1024
+VMEM_BYTES = 16 * 1024 * 1024
 
 AROUND = sorted(
     (
@@ -32,7 +32,12 @@
 S_TILES = 3
 IX, IY, IZ, IH, IU, IV, IW, IE, IB, IR, IF, IS = range(12)
 I_TILES = 12
+FIELDS = (IX, IY, IZ, IH, IU, IV, IW, IE, IB, IF)
 GROUPS = 16
+READY = 8
+STAGES = {"z": (0, 4), "x": (32, 6), "y": (80, 6), "w": (128, 3)}
+PAIRS = 152
+STEPS = [16 * a + 4 * b + c for a in (-1, 0, 1) for b in (-1, 0, 1) for c in (-1, 0, 1)]
 OWN = [(x, y, z) for x in (1, 2) for y in (1, 2) for z in (1, 2)]
 GHOST = [
     (x, y, z)
@@ -97,7 +102,7 @@
         jnp.where(ahead, 1.0, 0.0).astype(jnp.bfloat16),
         preferred_element_type=F32,
     )
-    return jnp.where(live, before, -1.0)
+    return jnp.where(live, before, -100.0)
 
 
 def chosen(ranks, c, group):
@@ -109,9 +114,9 @@
     return jnp.broadcast_to(jnp.sum(tile, axis=1, keepdims=True), (8, LANES))
 
 
-def density_sum(owns, spread, sites, accs):
+def density_sum(owns, spread, sites, accs, keep):
     accs = list(accs)
-    for site in sites:
+    for index, site in enumerate(sites):
         j = J_TILES * site
         xj, yj, zj, mj = (spread[j + k] for k in (JX, JY, JZ, JM))
         for k, (x, y, z, h4) in enumerate(owns):
@@ -120,28 +125,41 @@
             dz = z - zj
             sq = dx * dx + dy * dy + dz * dz
             r4 = sq * lax.rsqrt(jnp.maximum(sq, 1e-30))
+            keep(index, k, r4)
             u = jnp.maximum(h4 - r4, 0.0)
             u2 = u * u
             accs[k] = accs[k] + (u2 * u2) * ((0.25 * h4 + r4) * mj)
     return accs
 
 
-def force_sum(own, spread, states, sites, acc):
-    x, y, z, h4, vx, vy, vz, e4, b, rho, fac, sound = own
+def closing_speed(own, other, sq):
+    x, y, z, _, vx, vy, vz, e4 = own[:8]
+    xj, yj, zj, uj, vj, wj, ej = other
+    app = (x - xj) * (vx - uj) + (y - yj) * (vy - vj) + (z - zj) * (vz - wj)
+    e = e4 + ej
+    return e * jnp.minimum(app, 0.0) / (sq + e * e)
+
+
+def motion_of(spread, site):
+    return [spread[J_TILES * site + k] for k in (JX, JY, JZ, JU, JV, JW, JE)]
+
+
+def force_sum(own, spread, states, pairs, acc):
+    x, y, z, h4, _, _, _, _, b, rho, fac, sound = own
     ax, ay, az = acc
-    for site in sites:
+    for site, r4, m in pairs:
         j = J_TILES * site
         s = S_TILES * site
         dx = x - spread[j + JX]
         dy = y - spread[j + JY]
         dz = z - spread[j + JZ]
-        sq = dx * dx + dy * dy + dz * dz
-        app = dx * (vx - spread[j + JU]) + dy * (vy - spread[j + JV]) + dz * (vz - spread[j + JW])
-        r4 = sq * lax.rsqrt(jnp.maximum(sq, 1e-30))
+        if r4 is None:
+            sq = dx * dx + dy * dy + dz * dz
+            r4 = sq * lax.rsqrt(jnp.maximum(sq, 1e-30))
+        if m is None:
+            m = closing_speed(own, motion_of(spread, site), r4 * r4)
         near = jnp.maximum(h4 - r4, 0.0)
         far = jnp.maximum(spread[j + JH] - r4, 0.0)
-        e = e4 + spread[j + JE]
-        m = e * jnp.minimum(app, 0.0) / (sq + e * e)
         visc = m * (m - (sound + states[s + JS])) / (rho + states[s + JR])
         g_near = (near * near) * (near * (b * spread[j + JM]))
         g_far = (far * far) * (far * spread[j + JB])
@@ -156,8 +174,19 @@
     gx, gy, gz = 3 * (c // 4), 3 * ((c // 2) % 2), 3 * (c % 2)
     z_side = [flat(x, y, gz) for x in (1, 2) for y in (1, 2)]
     x_side = [flat(gx, y, z) for y in (1, 2) for z in (1, 2, gz)]
-    y_side = [flat(x, gy, z) for x in (1, 2, gx) for z in (1, 2, gz)]
-    return {"z": z_side, "x": x_side, "y": y_side}[which]
+    y_side = [flat(x, gy, z) for x in (1, 2) for z in (1, 2, gz)]
+    w_side = [flat(gx, gy, z) for z in (1, 2, gz)]
+    return {"z": z_side, "x": x_side, "y": y_side, "w": w_side}[which]
+
+
+def stage_of(step):
+    if step[1]:
+        return "w" if step[0] else "y"
+    return "x" if step[0] else "z"
+
+
+def outside(place):
+    return tuple(0 if k in (1, 2) else 1 for k in place)
 
 
 def own_sites():
@@ -206,6 +235,8 @@
     gas,
     ranks,
     density,
+    roots,
+    slopes,
     offsets,
     velocities,
     smoothing,
@@ -217,6 +248,8 @@
     own_states,
     sums,
     picked,
+    columns,
+    own_roots,
     load_sem,
     send_sem,
     recv_sem,
@@ -262,6 +295,14 @@
         motion_tiles(cells, spread, x, y, z)
     ranks[...] = ranks_of(active[...])
 
+    def spread_columns(c, targets):
+        for target in targets:
+            source = FIELDS.index(target)
+            for group in range(GROUPS):
+                particles[I_TILES * (GROUPS * c + group) + target] = jnp.broadcast_to(
+                    columns[c, 8 * group : 8 * group + 8, source : source + 1], (8, LANES)
+                )
+
     for c, (x, y, z) in enumerate(OWN):
         tile = cells[x, y, z]
         h4 = 4.0 * tile[7:8]
@@ -276,75 +317,68 @@
         picked[10:16, :] = jnp.zeros((6, LANES), F32)
         places = lax.broadcasted_iota(jnp.int32, (LANES, LANES), 0).astype(F32)
         found = places == jnp.broadcast_to(ranks[c : c + 1], (LANES, LANES))
-        columns = lax.dot_general(
+        columns[c] = lax.dot_general(
             jnp.where(found, 1.0, 0.0),
             picked[...],
             (((1,), (1,)), ((), ())),
             precision=lax.Precision.HIGHEST,
             preferred_element_type=F32,
         )
-        for group in range(GROUPS):
-            at = I_TILES * (GROUPS * c + group)
-            for source, target in enumerate((IX, IY, IZ, IH, IU, IV, IW, IE, IB, IF)):
-                particles[at + target] = jnp.broadcast_to(
-                    columns[8 * group : 8 * group + 8, source : source + 1], (8, LANES)
-                )
+        spread_columns(c, (IX, IY, IZ, IH))
 
     def density_inputs(t):
         at = I_TILES * t
         return [particles[at + k] for k in (IX, IY, IZ, IH)]
 
-    def inner_density(quad, carry):
-        zero = jnp.zeros((8, LANES), F32)
-        some = [4 * quad + k for k in range(4)]
-        accs = density_sum([density_inputs(t) for t in some], spread, own_sites(), [zero] * 4)
+    zero = jnp.zeros((8, LANES), F32)
+
+    def density_part(c, half, sites, first, target, fresh):
+        some = [GROUPS * c + 8 * half + k for k in range(8)]
+
+        def keep(index, k, value):
+            target[first + index, pl.ds(pl.multiple_of(64 * half, 64) + 8 * k, 8), :] = value
+
+        accs = density_sum(
+            [density_inputs(t) for t in some],
+            spread,
+            sites,
+            [zero] * 8 if fresh else [sums[t] for t in some],
+            keep,
+        )
         for t, acc in zip(some, accs):
             sums[t] = acc
+
+    def inner_density(part, carry):
+        c = part // 2
+        density_part(c, part % 2, own_sites(), 8 * c, own_roots, True)
         return carry
 
-    lax.fori_loop(0, 2 * GROUPS, inner_density, 0)
-
-    for which in ("z", "x", "y"):
-        axis = {"z": 2, "x": 0, "y": 1}[which]
-        later = {"z": (0, 1), "x": (1,), "y": ()}[which]
+    lax.fori_loop(0, GROUPS, inner_density, 0)
+
+    for which, (base, per_cell) in STAGES.items():
         for step in AROUND:
-            if step[axis] and not any(step[k] for k in later):
+            if stage_of(step) == which:
                 copies[step].wait_recv()
         for x, y, z in GHOST:
-            cell = (x, y, z)
-            if cell[axis] in (0, 3) and not any(cell[k] in (0, 3) for k in later):
+            if stage_of(outside((x, y, z))) == which:
                 place_tiles(cells, spread, x, y, z)
-
         for c in range(8):
-            sites = ghost_sites(c, which)
-
-            def outer_density(quad, carry, c=c, sites=sites):
-                some = [GROUPS * c + 4 * quad + k for k in range(4)]
-                accs = density_sum(
-                    [density_inputs(t) for t in some], spread, sites, [sums[t] for t in some]
-                )
-                for t, acc in zip(some, accs):
-                    sums[t] = acc
+
+            def outer_density(half, carry, c=c, which=which, first=base + per_cell * c):
+                density_part(c, half, ghost_sites(c, which), first, roots, False)
                 return carry
 
-            lax.fori_loop(0, GROUPS // 4, outer_density, 0)
-
-    def settle(c, carry):
-        total = jnp.zeros((8, LANES), F32)
+            lax.fori_loop(0, 2, outer_density, 0)
+
+    for c in range(8):
+        spread_columns(c, (IB,))
+        total = zero
         for group in range(GROUPS):
             t = GROUPS * c + group
-            at = I_TILES * t
-            mask = chosen(ranks, c, group)
-            rho = across(sums[t]) * (0.1 * particles[at + IB])
-            total = total + jnp.where(mask, rho, 0.0)
-            fac = particles[at + IF] * jnp.exp(jnp.log(rho) * (-1.0 / 3.0))
-            particles[at + IR] = rho
-            particles[at + IF] = 8.0 * fac
-            particles[at + IS] = jnp.sqrt((5.0 / 3.0) * fac * rho)
-        density[pl.ds(c, 1), :] = jnp.sum(total, axis=0, keepdims=True)
-        return carry
-
-    lax.fori_loop(0, 8, settle, 0)
+            rho = across(sums[t]) * (0.1 * particles[I_TILES * t + IB])
+            particles[I_TILES * t + IR] = rho
+            total = total + jnp.where(chosen(ranks, c, group), rho, 0.0)
+        density[c : c + 1, :] = jnp.sum(total, axis=0, keepdims=True)
     rho = jnp.where(active[...] == 1, density[...], prior[...])
     density[...] = rho
     fac = entropy[...] * jnp.exp(jnp.log(rho) * (-1.0 / 3.0))
@@ -353,38 +387,85 @@
         gas[x, y, z, 1:2, :] = fac[c : c + 1]
     copies2 = send_all(gas, sizes, send2_sem, recv2_sem)
 
+    for c in range(8):
+        spread_columns(c, (IU, IV, IW, IE, IF))
+
+    def settle(t, carry):
+        at = I_TILES * t
+        rho_i = particles[at + IR]
+        fac_i = particles[at + IF] * jnp.exp(jnp.log(rho_i) * (-1.0 / 3.0))
+        particles[at + IF] = 8.0 * fac_i
+        particles[at + IS] = jnp.sqrt((5.0 / 3.0) * fac_i * rho_i)
+        return carry
+
+    lax.fori_loop(0, 8 * GROUPS, settle, 0, unroll=8)
+
     for c, (x, y, z) in enumerate(OWN):
         state_tiles(rho[c : c + 1], fac[c : c + 1], own_states, flat(x, y, z))
 
     def inner_force(t, carry):
-        at = I_TILES * t
-        zero = jnp.zeros((8, LANES), F32)
+        c, group = t // READY, t % READY
+        at = I_TILES * (GROUPS * c + group)
+        rows = pl.ds(pl.multiple_of(8 * group, 8), 8)
         acc = force_sum(
             [particles[at + k] for k in range(I_TILES)],
             spread,
             own_states,
-            own_sites(),
+            [(site, own_roots[8 * c + k, rows, :], None) for k, site in enumerate(own_sites())],
             (zero, zero, zero),
         )
         for d in range(3):
             partial[3 * t + d] = acc[d]
         return carry
 
-    lax.fori_loop(0, 8 * GROUPS, inner_force, 0, unroll=2)
+    lax.fori_loop(0, 8 * READY, inner_force, 0)
     for x, y, z in GHOST:
         motion_tiles(cells, spread, x, y, z)
+    for c in range(8):
+        pairs = [
+            (site, base + per_cell * c + k)
+            for which, (base, per_cell) in STAGES.items()
+            for k, site in enumerate(ghost_sites(c, which))
+        ]
+
+        def slope(two, carry, c=c, pairs=pairs):
+            owns = [
+                [particles[I_TILES * (GROUPS * c + 2 * two + k) + f] for f in range(8)]
+                for k in range(2)
+            ]
+            for site, pair in pairs:
+                other = motion_of(spread, site)
+                for k, own in enumerate(owns):
+                    rows = pl.ds(pl.multiple_of(16 * two, 16) + 8 * k, 8)
+                    r4 = roots[pair, rows, :]
+                    slopes[pair, rows, :] = closing_speed(own, other, r4 * r4)
+            return carry
+
+        lax.fori_loop(0, READY // 2, slope, 0)
     for step in AROUND:
         copies[step].wait_send()
         copies2[step].wait()
 
 
 def force_kernel(
-    spread, particles, partial, gas, ranks, density_in, density, accel, states, sums, counts
+    spread,
+    particles,
+    partial,
+    gas,
+    ranks,
+    density_in,
+    roots,
+    slopes,
+    density,
+    accel,
+    states,
+    sums,
+    counts,
 ):
     density[...] = density_in[...]
     last = jnp.max(ranks[...], axis=1, keepdims=True)
     for c in range(8):
-        counts[c] = (jnp.max(last[c : c + 1]) + 1.0).astype(jnp.int32)
+        counts[c] = (jnp.maximum(jnp.max(last[c : c + 1]), -1.0) + 8.0).astype(jnp.int32) // 8
 
     def prepare(site, carry):
         state_tiles(gas[site, 0:1, :], gas[site, 1:2, :], states, site)
@@ -393,39 +474,70 @@
     lax.fori_loop(0, 64, prepare, 0, unroll=4)
 
     zero = jnp.zeros((8, LANES), F32)
-    for c in range(8):
-        groups = (counts[c] + 7) // 8
-        sites = [site for which in ("z", "x", "y") for site in ghost_sites(c, which)]
-
-        def group_step(group, inner, c=c, sites=sites):
-            t = GROUPS * c + group
-            at = I_TILES * t
+    nothing = (zero, zero, zero)
+
+    def late_cell(c, carry):
+        here = flat(1 + c // 4, 1 + (c // 2) % 2, 1 + c % 2)
+
+        def late_group(group, found):
+            at = I_TILES * (GROUPS * c + group)
             acc = force_sum(
                 [particles[at + k] for k in range(I_TILES)],
                 spread,
                 states,
-                sites,
+                [(here + step, None, None) for step in STEPS],
+                nothing,
+            )
+            mask = chosen(ranks, c, group)
+            return tuple(
+                total + jnp.where(mask, across(part), 0.0) for total, part in zip(found, acc)
+            )
+
+        found = lax.fori_loop(READY, jnp.maximum(counts[c], READY), late_group, nothing)
+        for d in range(3):
+            accel[pl.ds(8 * d + c, 1), :] = jnp.sum(found[d], axis=0, keepdims=True)
+        return carry
+
+    lax.fori_loop(0, 8, late_cell, 0)
+    sums[...] = jnp.zeros(sums.shape, F32)
+
+    def fold(c, group, totals):
+        mask = chosen(ranks, c, group)
+        at = 3 * (READY * c + jnp.maximum(group, 0))
+        return tuple(
+            total + jnp.where(mask, across(sums[at + d]), 0.0) for d, total in enumerate(totals)
+        )
+
+    totals = []
+    for c in range(8):
+        pairs = [
+            (site, base + per_cell * c + k)
+            for which, (base, per_cell) in STAGES.items()
+            for k, site in enumerate(ghost_sites(c, which))
+        ]
+
+        def group_step(group, found, c=c, pairs=pairs):
+            found = fold(c, group - 1, found)
+            at = I_TILES * (GROUPS * c + group)
+            t = READY * c + group
+            rows = pl.ds(pl.multiple_of(8 * group, 8), 8)
+            acc = force_sum(
+                [particles[at + k] for k in range(I_TILES)],
+                spread,
+                states,
+                [(site, roots[pair, rows, :], slopes[pair, rows, :]) for site, pair in pairs],
                 tuple(partial[3 * t + d] for d in range(3)),
             )
             for d in range(3):
-                sums[3 * group + d] = acc[d]
-            return inner
-
-        lax.fori_loop(0, groups, group_step, 0)
-
-        def fold(quad, totals, c=c):
-            for k in range(4):
-                group = 4 * quad + k
-                mask = chosen(ranks, c, group)
-                totals = tuple(
-                    total + jnp.where(mask, across(sums[3 * group + d]), 0.0)
-                    for d, total in enumerate(totals)
-                )
-            return totals
-
-        totals = lax.fori_loop(0, (groups + 3) // 4, fold, (zero, zero, zero))
+                sums[3 * t + d] = acc[d]
+            return found
+
+        totals.append(lax.fori_loop(0, jnp.minimum(counts[c], READY), group_step, nothing))
+    for c in range(8):
+        found = fold(c, jnp.minimum(counts[c], READY) - 1, totals[c])
         for d in range(3):
-            accel[8 * d + c : 8 * d + c + 1, :] = 0.25 * jnp.sum(totals[d], axis=0, keepdims=True)
+            row = slice(8 * d + c, 8 * d + c + 1)
+            accel[row, :] = 0.25 * (accel[row, :] + jnp.sum(found[d], axis=0, keepdims=True))
 
 
 def vmem(count):
@@ -439,18 +551,20 @@
 def body(sizes, *args):
     rows = [pltpu.with_memory_space_constraint(a.reshape(-1, LANES), pltpu.HBM) for a in args]
     cell_rows = jax.ShapeDtypeStruct((8, LANES), F32)
-    spread, particles, partial, gas, ranks, density = pl.pallas_call(
+    spread, particles, partial, gas, ranks, density, roots, slopes = pl.pallas_call(
         functools.partial(gather_kernel, sizes),
         out_shape=(
             tiles(64 * J_TILES),
             tiles(8 * GROUPS * I_TILES),
-            tiles(8 * GROUPS * 3),
+            tiles(8 * READY * 3),
             jax.ShapeDtypeStruct((4, 4, 4, 2, LANES), F32),
             cell_rows,
             cell_rows,
+            jax.ShapeDtypeStruct((PAIRS, LANES, LANES), F32),
+            jax.ShapeDtypeStruct((PAIRS, 8 * READY, LANES), F32),
         ),
         in_specs=[pl.BlockSpec(memory_space=pltpu.HBM)] * 7,
-        out_specs=tuple(vmem(6)),
+        out_specs=tuple(vmem(8)),
         scratch_shapes=[
             pltpu.VMEM((24, LANES), F32),
             pltpu.VMEM((24, LANES), F32),
@@ -463,6 +577,8 @@
             pltpu.VMEM((64 * S_TILES, 8, LANES), F32),
             pltpu.VMEM((8 * GROUPS, 8, LANES), F32),
             pltpu.VMEM((16, LANES), F32),
+            pltpu.VMEM((8, LANES, 16), F32),
+            pltpu.VMEM((64, LANES, LANES), F32),
             pltpu.SemaphoreType.DMA((7,)),
             pltpu.SemaphoreType.DMA((COUNT,)),
             pltpu.SemaphoreType.DMA((COUNT,)),
@@ -476,15 +592,15 @@
     density, accel = pl.pallas_call(
         force_kernel,
         out_shape=(cell_rows, jax.ShapeDtypeStruct((24, LANES), F32)),
-        in_specs=vmem(6),
+        in_specs=vmem(8),
         out_specs=tuple(vmem(2)),
         scratch_shapes=[
             pltpu.VMEM((64 * S_TILES, 8, LANES), F32),
-            pltpu.VMEM((GROUPS * 3, 8, LANES), F32),
+            pltpu.VMEM((8 * READY * 3, 8, LANES), F32),
             pltpu.SMEM((8,), jnp.int32),
         ],
         compiler_params=pltpu.CompilerParams(vmem_limit_bytes=VMEM_BYTES),
-    )(spread, particles, partial, gas.reshape(64, 2, LANES), ranks, density)
+    )(spread, particles, partial, gas.reshape(64, 2, LANES), ranks, density, roots, slopes)
     return density.reshape(2, 2, 2, LANES), accel.reshape(3, 2, 2, 2, LANES)
 
 

time: 52.5 us -> 46.1 us (0.88)
  the two profiles are of different devices: /device:TPU:1 before, /device:TPU:24 now
where the time goes in v5:
time: 46.1 us; the launch traced here: 46 us
  Pallas kernels  45.3 us (98%)
  between operations  0.64 us (1%)
    pallas_call x1, Pallas kernels, body(): pl.pallas_call(functools.partial(gather_kernel, sizes), out_shape=(tiles(...  38.3 us
    pallas_call x1, Pallas kernels, body(): pl.pallas_call(force_kernel, out_shape=(cell_rows, jax.ShapeDtypeStruct((...  6.97 us

profile of v5, /device:TPU:24, one launch (start us, length us, event | category | flops | bytes accessed | tf_op | source)
XLA Modules:
  0.0 46.0 jit_solution(2321031129805034152)
XLA Ops:
  0.6 38.3 %shard_map.86 = (f32[640,8,128]{2,1,0:T(8,128)S(1)}, f32[1536,8,128]{2,1,0:T(8,128)S(1)}, f32[192,8,128]{2,1,0:T(8,128)S(1)}, f32[4,4,4,2,128]{4,3,2,1,0:T(2,128...) custom-call(f32[24,128]{1,0:T(8,128)} %bitcast.11, ...), custom_call_target="tpu_custom_call" | custom-call | tf_op jit(solution)/shard_map/pallas_call | solution.py:554
  39.0 7.0 %shard_map.87 = (f32[8,128]{1,0:T(8,128)}, f32[24,128]{1,0:T(8,128)}) custom-call(f32[640,8,128]{2,1,0:T(8,128)S(1)} %get-tuple-element.12.spread, f32[1536,8,128]{2,1,0:T(8,128)S(1)} %get-tuple-element.13.particles, f32[192,8,128]{2,1,0:T(8,128)S(1)} %get-tuple-element.14.partial, f32[64,2,128]{2,1,0:T(2,128)S(1)} %bitcast.10, ...), custom_call_target="tpu_custom_call" | custom-call | tf_op jit(solution)/shard_map/pallas_call | solution.py:592
